TPU v7x, 32 devices: a whole 2x2x4 slice. The times are simulated.
32 devices in a mesh: dev: 32 (over z, y, x, core).
Axes of the slice: x: 2, y: 2, z: 4, core: 2. Of those that a mesh axis runs over, the one named last changes fastest.
Arguments:
- tokens: bfloat16 [65536, 768], P('dev'), may hold values from -6 to 6
- cotangent: bfloat16 [65536, 768], P('dev'), may hold values from -6 to 6
- in_weight: bfloat16 [768, 3352], P('dev'), may hold values from -0.21875 to 0.21875
- out_weight: bfloat16 [1536, 768], P('dev'), may hold values from -0.3125 to 0.3125
- conv_weight: bfloat16 [1792, 4], P('dev'), may hold values from -3 to 3
- conv_bias: bfloat16 [1792], P('dev'), may hold values from -3 to 3
- norm_gain: bfloat16 [768], P('dev'), may hold values from 0.5 to 1.5
- gated_gain: bfloat16 [1536], P('dev'), may hold values from 0.5 to 1.5
- head_params: float32 [3, 24], replicated, may hold values from -7 to 3, as said below
- group_length: int32 [256], P('dev'), may hold values from 0 to 256, as said below
- group_first: int32 [256], P('dev'), may hold values from 0 to 1, as said below
Outputs:
- block_out: bfloat16 [65536, 768], P('dev')
- token_grad: float32 [65536, 768], P('dev')
- in_weight_grad: float32 [768, 3352], P('dev')
- out_weight_grad: float32 [1536, 768], P('dev')
- conv_weight_grad: float32 [1792, 4], P('dev')
- conv_bias_grad: float32 [1792], P('dev')
- norm_gain_grad: float32 [768], P('dev')
- gated_gain_grad: float32 [1536], P('dev')
- head_grad: float32 [3, 24], replicated
Inputs may be any that keep to these rules, and one draw needn't show every extreme that they name: `head_params`: step bias per head between inverse softplus of 0.001 and of 0.1; log decay between 0 and log 16; skip factor between 0.5 and 1.5. `group_length`: each device's first group is full. A group's live tokens come first in it. `group_first`: A sequence spans one or two groups of one device; a continuing group stands at an odd group place of its device, follows a full group, and has live tokens. Each device's first group begins a sequence.
All inputs are finite; a program needn't handle non-finite values.
Results may differ from a plain program's by a relative error of at most 0.007.
Values may be sent and summed in bfloat16 or wider, within the bound.
A program may use at most 384 MiB of HBM per device.

v0:
```python
import jax
import jax.numpy as jnp
from jax import lax
from jax.sharding import PartitionSpec as P

HEADS = 24
HEAD_DIM = 64
STATE = 128
KERNEL = 4
GROUP = 256
INNER = 1536
CONV_CH = 1792


EPSILON = 1e-05


def rounded(value):
    kept = lax.optimization_barrier(value.astype(jnp.bfloat16)).astype(jnp.float32)
    return value + lax.stop_gradient(kept - value)


def exact_dot(left, right):
    return jnp.dot(left, right, precision=lax.Precision.HIGHEST)


def group_mixer(decay_rate):

    def advance(state, pieces):
        c_rows, b_rows, x_heads, step_size, carry_on = pieces
        running = jnp.cumsum(step_size * decay_rate[None, :], axis=0)
        places = jnp.arange(c_rows.shape[0])
        causal = (places[:, None] >= places[None, :])[:, :, None]
        spread = running[:, None, :] - running[None, :, :]
        decay = jnp.where(causal, jnp.exp(jnp.where(causal, spread, 0.0)), 0.0)
        scores = exact_dot(c_rows, b_rows.T)
        mixing = rounded(
            jnp.transpose(scores[:, :, None] * decay * step_size[None, :, :], (2, 0, 1))
        )
        inner = jnp.einsum("hts,shp->thp", mixing, x_heads, precision=lax.Precision.HIGHEST)
        start = state * carry_on
        outer = jnp.exp(running)[:, :, None] * jnp.einsum(
            "tn,hnp->thp", c_rows, rounded(start), precision=lax.Precision.HIGHEST
        )
        to_end = jnp.exp(running[-1][None, :] - running) * step_size
        weighted = rounded(x_heads * to_end[:, :, None])
        fresh = jnp.einsum("sn,shp->hnp", b_rows, weighted, precision=lax.Precision.HIGHEST)
        new_state = jnp.exp(running[-1])[:, None, None] * start + fresh
        return (new_state, inner + outer)

    return advance


def input_norm(tok, norm_g):
    return tok * lax.rsqrt(jnp.mean(tok * tok, axis=1, keepdims=True) + EPSILON) * norm_g


def middle(projected, conv_w, conv_b, gated_g, head_p, firsts):
    total_rows = projected.shape[0]
    group_count = total_rows // GROUP
    slot_place = jnp.arange(total_rows, dtype=jnp.int32) % GROUP
    seq_place = slot_place + GROUP * (1 - jnp.repeat(firsts, GROUP))
    gate_part = projected[:, :INNER]
    conv_in = projected[:, INNER : INNER + CONV_CH]
    raw_step = projected[:, INNER + CONV_CH :]
    mixed_conv = conv_b + conv_in * conv_w[:, KERNEL - 1]
    for lag in range(1, KERNEL):
        earlier = jnp.concatenate([jnp.zeros((lag, CONV_CH), jnp.float32), conv_in[:-lag]], axis=0)
        keep = (seq_place >= lag).astype(jnp.float32)[:, None]
        mixed_conv = mixed_conv + conv_w[:, KERNEL - 1 - lag] * earlier * keep
    activated = rounded(jax.nn.silu(mixed_conv))
    x_heads = activated[:, :INNER].reshape(total_rows, HEADS, HEAD_DIM)
    b_rows = activated[:, INNER : INNER + STATE]
    c_rows = activated[:, INNER + STATE :]
    step_size = jax.nn.softplus(raw_step + head_p[2][None, :])
    decay_rate = -jnp.exp(head_p[0])
    carry_on = (1 - firsts).astype(jnp.float32)
    pieces = (
        c_rows.reshape(group_count, GROUP, STATE),
        b_rows.reshape(group_count, GROUP, STATE),
        x_heads.reshape(group_count, GROUP, HEADS, HEAD_DIM),
        step_size.reshape(group_count, GROUP, HEADS),
        carry_on,
    )
    initial = jnp.zeros((HEADS, STATE, HEAD_DIM), jnp.float32)
    final_state, mixer = lax.scan(jax.checkpoint(group_mixer(decay_rate)), initial, pieces)
    mixer = mixer.reshape(total_rows, HEADS, HEAD_DIM) + head_p[1][None, :, None] * x_heads
    gated = mixer.reshape(total_rows, INNER) * jax.nn.silu(gate_part)
    return gated * lax.rsqrt(jnp.mean(gated * gated, axis=1, keepdims=True) + EPSILON) * gated_g


def body(
    tokens,
    cotangent,
    in_weight,
    out_weight,
    conv_weight,
    conv_bias,
    norm_gain,
    gated_gain,
    head_params,
    group_length,
    group_first,
):
    token_float = tokens.astype(jnp.float32)
    row_count = tokens.shape[0]
    slot_place = jnp.arange(row_count, dtype=jnp.int32) % GROUP
    live_mask = (slot_place < jnp.repeat(group_length, GROUP)).astype(jnp.float32)[:, None]
    gathered = (
        lax.all_gather(in_weight, "dev", axis=0, tiled=True),
        lax.all_gather(out_weight, "dev", axis=0, tiled=True),
        lax.all_gather(conv_weight, "dev", axis=0, tiled=True),
        lax.all_gather(conv_bias, "dev", axis=0, tiled=True),
        lax.all_gather(norm_gain, "dev", axis=0, tiled=True),
        lax.all_gather(gated_gain, "dev", axis=0, tiled=True),
    )

    def run_forward(weight_set):
        normed, norm_pull = jax.vjp(input_norm, token_float, weight_set[4].astype(jnp.float32))
        normed_low = normed.astype(jnp.bfloat16)
        projected = jnp.dot(normed_low, weight_set[0], preferred_element_type=jnp.float32)

        def inner_part(proj, conv_w, conv_b, gated_g, head_p):
            return middle(proj, conv_w, conv_b, gated_g, head_p, group_first)

        gnormed, mid_pull = jax.vjp(
            inner_part,
            projected,
            weight_set[2].astype(jnp.float32),
            weight_set[3].astype(jnp.float32),
            weight_set[5].astype(jnp.float32),
            head_params,
        )
        return (normed_low, norm_pull, mid_pull, gnormed.astype(jnp.bfloat16))

    normed_low, norm_pull, mid_pull, gnormed_low = run_forward(gathered)
    branch = jnp.dot(gnormed_low, gathered[1], preferred_element_type=jnp.float32)
    block_out = (token_float + live_mask * branch).astype(jnp.bfloat16)
    backed = (
        lax.all_gather(in_weight, "dev", axis=0, tiled=True),
        lax.all_gather(out_weight, "dev", axis=0, tiled=True),
        lax.all_gather(conv_weight, "dev", axis=0, tiled=True),
        lax.all_gather(conv_bias, "dev", axis=0, tiled=True),
        lax.all_gather(norm_gain, "dev", axis=0, tiled=True),
        lax.all_gather(gated_gain, "dev", axis=0, tiled=True),
    )
    normed_low, norm_pull, mid_pull, gnormed_low = run_forward(backed)
    picked = cotangent * live_mask.astype(jnp.bfloat16)
    out_grad = jnp.dot(gnormed_low.T, picked, preferred_element_type=jnp.float32)
    grad_gnormed = jnp.dot(picked, backed[1].T, preferred_element_type=jnp.float32)
    grad_proj, grad_conv_w, grad_conv_b, grad_gated_g, grad_heads = mid_pull(grad_gnormed)
    grad_proj_low = grad_proj.astype(jnp.bfloat16)
    in_grad = jnp.dot(normed_low.T, grad_proj_low, preferred_element_type=jnp.float32)
    grad_normed = jnp.dot(grad_proj_low, backed[0].T, preferred_element_type=jnp.float32)
    grad_tokens, grad_norm_g = norm_pull(grad_normed)
    token_grad = cotangent.astype(jnp.float32) + grad_tokens
    owned = (
        lax.psum_scatter(in_grad, "dev", scatter_dimension=0, tiled=True),
        lax.psum_scatter(out_grad, "dev", scatter_dimension=0, tiled=True),
        lax.psum_scatter(grad_conv_w, "dev", scatter_dimension=0, tiled=True),
        lax.psum_scatter(grad_conv_b, "dev", scatter_dimension=0, tiled=True),
        lax.psum_scatter(grad_norm_g, "dev", scatter_dimension=0, tiled=True),
        lax.psum_scatter(grad_gated_g, "dev", scatter_dimension=0, tiled=True),
    )
    head_total = lax.psum(grad_heads, "dev")
    return (
        block_out,
        token_grad,
        owned[0],
        owned[1],
        owned[2],
        owned[3],
        owned[4],
        owned[5],
        head_total,
    )


def solution(mesh):
    placed = (
        P("dev", None),
        P("dev", None),
        P("dev", None),
        P("dev", None),
        P("dev", None),
        P("dev"),
        P("dev"),
        P("dev"),
        P(),
        P("dev"),
        P("dev"),
    )
    return jax.shard_map(
        body,
        mesh=mesh,
        in_specs=placed,
        out_specs=(
            P("dev", None),
            P("dev", None),
            P("dev", None),
            P("dev", None),
            P("dev", None),
            P("dev"),
            P("dev"),
            P("dev"),
            P(),
        ),
        check_vma=False,
    )
```

profile of v0, /device:TPU:0, one launch (start us, length us, event | category | flops | bytes accessed | tf_op | source)
XLA Modules:
  0.0 2732.1 jit_solution(12416390228265138880)
XLA Ops:
  14.9 42.3 %all-reduce.30 = (bf16[768]{0:T(1024)(128)(2,1)S(1)}, bf16[1792]{0:T(1024)(128)(2,1)S(1)}, bf16[1536]{0:T(1024)(128)(2,1)S(1)}) all-reduce(bf16[768]{0:T(1024)(128)(2,1)S(1)} %dynamic-update-slice, bf16[1792]{0:T(1024)(128)(2,1)S(1)} %dynamic-update-slice.1, bf16[1536]{0:T(1024)(128)(2,1)S(1)} %dynamic-update-slice.2), channel_id=1, replica_groups=mesh['dev'=32] {'dev'}, use_global_device_ids=true, to_apply=%add.21 | all-reduce | flops 4096 | bytes 16384
  61.1 40.2 %all-gather = bf16[32,56,4]{1,2,0:T(4,128)(2,1)S(1)} all-gather(bf16[1,56,4]{1,2,0:T(4,128)(2,1)} %bitcast.632), channel_id=1, replica_groups=mesh['dev'=32] {'dev'}, dimensions={0}, use_global_device_ids=true | all-gather | bytes 14784 | tf_op jit(solution)/shard_map/all_gather | solution.py:112
  102.9 19.1 fusion.173
  122.0 13.5 slice.189
  135.5 13.2 slice.187
  148.7 13.0 slice.185
  161.7 27.1 fusion.167
  188.9 11.9 subtract_add_fusion.31
  200.7 11.2 slice.190
  216.5 15.4 copy.313
  231.9 13.3 copy.235
  253.9 514.8 %while.58 = (s32[]{:T(128)}, f32[24,128,64]{1,2,0:T(8,128)S(1)}, f32[8,256,24,64]{1,0,3,2:T(8,128)}, f32[8,24,128,64]{2,3,1,0:T(8,128)}, f32[8,256,24]{1,2,0:T(8...) while((s32[]{:T(128)}, f32[24,128,64]{1,2,0:T(8,128)S(1)}, ...), condition=%wide.region_9.10_spmd.clone, body=%wide.region_6.9_spmd.clone.sunk | while | flops 2545115136 | bytes 32634740 | solution.py:86
  282.5 35.8 %dynamic_update_slice.77 = f32[8,256,24,64]{1,0,3,2:T(8,128)} dynamic-update-slice(f32[8,256,24,64]{1,0,3,2:T(8,128)} %get-tuple-element.1422, f32[1,256,24,64]{1,0,3,2:T(1,128)S(1)} %copy.389, s32[]{:T(128)S(6)} %copy.417, s32[]{:T(128)} %constant.175.clone.1..sunk.1, s32[]{:T(128)} %constant.175.clone.1..sunk.1, s32[]{:T(128)} %constant.175.clone.1..sunk.1) | dynamic-update-slice | bytes 3145732 | tf_op jit(solution)/shard_map/jvp()/while/body/jit(dynamic_update_index_in_dim)/dynamic_update_slice | solution.py:86
  346.8 35.8 %dynamic_update_slice.77 = f32[8,256,24,64]{1,0,3,2:T(8,128)} dynamic-update-slice(f32[8,256,24,64]{1,0,3,2:T(8,128)} %get-tuple-element.1422, f32[1,256,24,64]{1,0,3,2:T(1,128)S(1)} %copy.389, s32[]{:T(128)S(6)} %copy.417, s32[]{:T(128)} %constant.175.clone.1..sunk.1, s32[]{:T(128)} %constant.175.clone.1..sunk.1, s32[]{:T(128)} %constant.175.clone.1..sunk.1) | dynamic-update-slice | bytes 3145732 | tf_op jit(solution)/shard_map/jvp()/while/body/jit(dynamic_update_index_in_dim)/dynamic_update_slice | solution.py:86
  411.2 35.8 %dynamic_update_slice.77 = f32[8,256,24,64]{1,0,3,2:T(8,128)} dynamic-update-slice(f32[8,256,24,64]{1,0,3,2:T(8,128)} %get-tuple-element.1422, f32[1,256,24,64]{1,0,3,2:T(1,128)S(1)} %copy.389, s32[]{:T(128)S(6)} %copy.417, s32[]{:T(128)} %constant.175.clone.1..sunk.1, s32[]{:T(128)} %constant.175.clone.1..sunk.1, s32[]{:T(128)} %constant.175.clone.1..sunk.1) | dynamic-update-slice | bytes 3145732 | tf_op jit(solution)/shard_map/jvp()/while/body/jit(dynamic_update_index_in_dim)/dynamic_update_slice | solution.py:86
  475.5 35.8 %dynamic_update_slice.77 = f32[8,256,24,64]{1,0,3,2:T(8,128)} dynamic-update-slice(f32[8,256,24,64]{1,0,3,2:T(8,128)} %get-tuple-element.1422, f32[1,256,24,64]{1,0,3,2:T(1,128)S(1)} %copy.389, s32[]{:T(128)S(6)} %copy.417, s32[]{:T(128)} %constant.175.clone.1..sunk.1, s32[]{:T(128)} %constant.175.clone.1..sunk.1, s32[]{:T(128)} %constant.175.clone.1..sunk.1) | dynamic-update-slice | bytes 3145732 | tf_op jit(solution)/shard_map/jvp()/while/body/jit(dynamic_update_index_in_dim)/dynamic_update_slice | solution.py:86
  539.8 35.8 %dynamic_update_slice.77 = f32[8,256,24,64]{1,0,3,2:T(8,128)} dynamic-update-slice(f32[8,256,24,64]{1,0,3,2:T(8,128)} %get-tuple-element.1422, f32[1,256,24,64]{1,0,3,2:T(1,128)S(1)} %copy.389, s32[]{:T(128)S(6)} %copy.417, s32[]{:T(128)} %constant.175.clone.1..sunk.1, s32[]{:T(128)} %constant.175.clone.1..sunk.1, s32[]{:T(128)} %constant.175.clone.1..sunk.1) | dynamic-update-slice | bytes 3145732 | tf_op jit(solution)/shard_map/jvp()/while/body/jit(dynamic_update_index_in_dim)/dynamic_update_slice | solution.py:86
  604.1 35.8 %dynamic_update_slice.77 = f32[8,256,24,64]{1,0,3,2:T(8,128)} dynamic-update-slice(f32[8,256,24,64]{1,0,3,2:T(8,128)} %get-tuple-element.1422, f32[1,256,24,64]{1,0,3,2:T(1,128)S(1)} %copy.389, s32[]{:T(128)S(6)} %copy.417, s32[]{:T(128)} %constant.175.clone.1..sunk.1, s32[]{:T(128)} %constant.175.clone.1..sunk.1, s32[]{:T(128)} %constant.175.clone.1..sunk.1) | dynamic-update-slice | bytes 3145732 | tf_op jit(solution)/shard_map/jvp()/while/body/jit(dynamic_update_index_in_dim)/dynamic_update_slice | solution.py:86
  668.4 35.8 %dynamic_update_slice.77 = f32[8,256,24,64]{1,0,3,2:T(8,128)} dynamic-update-slice(f32[8,256,24,64]{1,0,3,2:T(8,128)} %get-tuple-element.1422, f32[1,256,24,64]{1,0,3,2:T(1,128)S(1)} %copy.389, s32[]{:T(128)S(6)} %copy.417, s32[]{:T(128)} %constant.175.clone.1..sunk.1, s32[]{:T(128)} %constant.175.clone.1..sunk.1, s32[]{:T(128)} %constant.175.clone.1..sunk.1) | dynamic-update-slice | bytes 3145732 | tf_op jit(solution)/shard_map/jvp()/while/body/jit(dynamic_update_index_in_dim)/dynamic_update_slice | solution.py:86
  732.8 35.8 %dynamic_update_slice.77 = f32[8,256,24,64]{1,0,3,2:T(8,128)} dynamic-update-slice(f32[8,256,24,64]{1,0,3,2:T(8,128)} %get-tuple-element.1422, f32[1,256,24,64]{1,0,3,2:T(1,128)S(1)} %copy.389, s32[]{:T(128)S(6)} %copy.417, s32[]{:T(128)} %constant.175.clone.1..sunk.1, s32[]{:T(128)} %constant.175.clone.1..sunk.1, s32[]{:T(128)} %constant.175.clone.1..sunk.1) | dynamic-update-slice | bytes 3145732 | tf_op jit(solution)/shard_map/jvp()/while/body/jit(dynamic_update_index_in_dim)/dynamic_update_slice | solution.py:86
  768.7 15.4 copy.315
  784.2 14.3 multiply_reduce_fusion.11
  810.1 14.5 multiply_reduce_fusion.9
  830.5 507.2 %while.57 = (s32[]{:T(128)}, f32[24,128,64]{1,2,0:T(8,128)S(1)}, f32[8,256,24,64]{1,0,3,2:T(8,128)}, f32[8,256,24]{1,2,0:T(8,128)}, f32[1,24]{1,0:T(1,128)S(1)},...) while((s32[]{:T(128)}, f32[24,128,64]{1,2,0:T(8,128)S(1)}, ...), condition=%wide.region_4.5_spmd.clone, body=%wide.region_1.4_spmd.clone.sunk | while | flops 2544918528 | bytes 31061864 | solution.py:86
  858.1 35.8 %dynamic_update_slice.75 = f32[8,256,24,64]{1,0,3,2:T(8,128)} dynamic-update-slice(f32[8,256,24,64]{1,0,3,2:T(8,128)} %get-tuple-element.1463, f32[1,256,24,64]{1,0,3,2:T(1,128)S(1)} %copy.385, s32[]{:T(128)S(6)} %copy.428, s32[]{:T(128)} %constant.175.clone.1..sunk, s32[]{:T(128)} %constant.175.clone.1..sunk, s32[]{:T(128)} %constant.175.clone.1..sunk) | dynamic-update-slice | bytes 3145732 | tf_op jit(solution)/shard_map/jvp()/while/body/jit(dynamic_update_index_in_dim)/dynamic_update_slice | solution.py:86
  921.5 35.8 %dynamic_update_slice.75 = f32[8,256,24,64]{1,0,3,2:T(8,128)} dynamic-update-slice(f32[8,256,24,64]{1,0,3,2:T(8,128)} %get-tuple-element.1463, f32[1,256,24,64]{1,0,3,2:T(1,128)S(1)} %copy.385, s32[]{:T(128)S(6)} %copy.428, s32[]{:T(128)} %constant.175.clone.1..sunk, s32[]{:T(128)} %constant.175.clone.1..sunk, s32[]{:T(128)} %constant.175.clone.1..sunk) | dynamic-update-slice | bytes 3145732 | tf_op jit(solution)/shard_map/jvp()/while/body/jit(dynamic_update_index_in_dim)/dynamic_update_slice | solution.py:86
  984.9 35.8 %dynamic_update_slice.75 = f32[8,256,24,64]{1,0,3,2:T(8,128)} dynamic-update-slice(f32[8,256,24,64]{1,0,3,2:T(8,128)} %get-tuple-element.1463, f32[1,256,24,64]{1,0,3,2:T(1,128)S(1)} %copy.385, s32[]{:T(128)S(6)} %copy.428, s32[]{:T(128)} %constant.175.clone.1..sunk, s32[]{:T(128)} %constant.175.clone.1..sunk, s32[]{:T(128)} %constant.175.clone.1..sunk) | dynamic-update-slice | bytes 3145732 | tf_op jit(solution)/shard_map/jvp()/while/body/jit(dynamic_update_index_in_dim)/dynamic_update_slice | solution.py:86
  1048.3 35.8 %dynamic_update_slice.75 = f32[8,256,24,64]{1,0,3,2:T(8,128)} dynamic-update-slice(f32[8,256,24,64]{1,0,3,2:T(8,128)} %get-tuple-element.1463, f32[1,256,24,64]{1,0,3,2:T(1,128)S(1)} %copy.385, s32[]{:T(128)S(6)} %copy.428, s32[]{:T(128)} %constant.175.clone.1..sunk, s32[]{:T(128)} %constant.175.clone.1..sunk, s32[]{:T(128)} %constant.175.clone.1..sunk) | dynamic-update-slice | bytes 3145732 | tf_op jit(solution)/shard_map/jvp()/while/body/jit(dynamic_update_index_in_dim)/dynamic_update_slice | solution.py:86
  1111.6 35.8 %dynamic_update_slice.75 = f32[8,256,24,64]{1,0,3,2:T(8,128)} dynamic-update-slice(f32[8,256,24,64]{1,0,3,2:T(8,128)} %get-tuple-element.1463, f32[1,256,24,64]{1,0,3,2:T(1,128)S(1)} %copy.385, s32[]{:T(128)S(6)} %copy.428, s32[]{:T(128)} %constant.175.clone.1..sunk, s32[]{:T(128)} %constant.175.clone.1..sunk, s32[]{:T(128)} %constant.175.clone.1..sunk) | dynamic-update-slice | bytes 3145732 | tf_op jit(solution)/shard_map/jvp()/while/body/jit(dynamic_update_index_in_dim)/dynamic_update_slice | solution.py:86
  1175.0 35.8 %dynamic_update_slice.75 = f32[8,256,24,64]{1,0,3,2:T(8,128)} dynamic-update-slice(f32[8,256,24,64]{1,0,3,2:T(8,128)} %get-tuple-element.1463, f32[1,256,24,64]{1,0,3,2:T(1,128)S(1)} %copy.385, s32[]{:T(128)S(6)} %copy.428, s32[]{:T(128)} %constant.175.clone.1..sunk, s32[]{:T(128)} %constant.175.clone.1..sunk, s32[]{:T(128)} %constant.175.clone.1..sunk) | dynamic-update-slice | bytes 3145732 | tf_op jit(solution)/shard_map/jvp()/while/body/jit(dynamic_update_index_in_dim)/dynamic_update_slice | solution.py:86
  1238.4 35.8 %dynamic_update_slice.75 = f32[8,256,24,64]{1,0,3,2:T(8,128)} dynamic-update-slice(f32[8,256,24,64]{1,0,3,2:T(8,128)} %get-tuple-element.1463, f32[1,256,24,64]{1,0,3,2:T(1,128)S(1)} %copy.385, s32[]{:T(128)S(6)} %copy.428, s32[]{:T(128)} %constant.175.clone.1..sunk, s32[]{:T(128)} %constant.175.clone.1..sunk, s32[]{:T(128)} %constant.175.clone.1..sunk) | dynamic-update-slice | bytes 3145732 | tf_op jit(solution)/shard_map/jvp()/while/body/jit(dynamic_update_index_in_dim)/dynamic_update_slice | solution.py:86
  1301.8 35.8 %dynamic_update_slice.75 = f32[8,256,24,64]{1,0,3,2:T(8,128)} dynamic-update-slice(f32[8,256,24,64]{1,0,3,2:T(8,128)} %get-tuple-element.1463, f32[1,256,24,64]{1,0,3,2:T(1,128)S(1)} %copy.385, s32[]{:T(128)S(6)} %copy.428, s32[]{:T(128)} %constant.175.clone.1..sunk, s32[]{:T(128)} %constant.175.clone.1..sunk, s32[]{:T(128)} %constant.175.clone.1..sunk) | dynamic-update-slice | bytes 3145732 | tf_op jit(solution)/shard_map/jvp()/while/body/jit(dynamic_update_index_in_dim)/dynamic_update_slice | solution.py:86
  1337.7 15.5 copy.314
  1353.2 37.5 %multiply_reduce_fusion.8 = (f32[1536]{0:T(1024)}, f32[2048,1536]{0,1:T(8,128)}, f32[2048,1536]{0,1:T(8,128)}, f32[2048]{0:T(1024)}, f32[2048,1536]{0,1:T(8,128)}) fusion(f32[2048,1792]{0,1:T(8,128)} %subtract_add_fusion.31, f32[2048,3352]{0,1:T(8,128)} %fusion.173, f32[2048,1536]{0,1:T(8,128)} %copy-done.7, f32[2048]{0:T(1024)S(1)} %multiply_multiply_fusion.8, ...), kind=kLoop, calls=%fused_computation.222 | loop fusion | flops 78639616 | bytes 113289216 | tf_op jit(solution)/shard_map/transpose(jvp())/reduce_sum | solution.py:87
  1390.7 15.4 copy.316
  1414.9 946.9 %while.59 = (s32[]{:T(128)}, f32[24]{0:T(128)}, f32[24,128,64]{1,2,0:T(8,128)}, f32[8,256,128]{2,1,0:T(8,128)}, f32[8,256,128]{2,1,0:T(8,128)}, /*index=5*/f32[8...) while((s32[]{:T(128)}, f32[24]{0:T(128)}, ...), condition=%wide.region_26.27_spmd.clone, body=%wide.region_12.26_spmd.clone.sunk | while | flops 5793071104 | bytes 95370544 | solution.py:86
  1449.5 12.8 fusion.318
  1509.8 35.8 %dynamic_update_slice.80 = f32[8,256,24,64]{1,0,3,2:T(8,128)} dynamic-update-slice(f32[8,256,24,64]{1,0,3,2:T(8,128)} %get-tuple-element.1511, f32[1,256,24,64]{1,0,3,2:T(1,128)S(1)} %copy.401, s32[]{:T(128)S(6)} %sub.534, s32[]{:T(128)} %constant.175.clone.1..sunk.2, s32[]{:T(128)} %constant.175.clone.1..sunk.2, s32[]{:T(128)} %constant.175.clone.1..sunk.2) | dynamic-update-slice | bytes 3145732 | tf_op jit(solution)/shard_map/transpose(jvp())/while/body/jit(dynamic_update_index_in_dim)/dynamic_update_slice | solution.py:86
  1564.1 12.8 fusion.318
  1625.0 35.8 %dynamic_update_slice.80 = f32[8,256,24,64]{1,0,3,2:T(8,128)} dynamic-update-slice(f32[8,256,24,64]{1,0,3,2:T(8,128)} %get-tuple-element.1511, f32[1,256,24,64]{1,0,3,2:T(1,128)S(1)} %copy.401, s32[]{:T(128)S(6)} %sub.534, s32[]{:T(128)} %constant.175.clone.1..sunk.2, s32[]{:T(128)} %constant.175.clone.1..sunk.2, s32[]{:T(128)} %constant.175.clone.1..sunk.2) | dynamic-update-slice | bytes 3145732 | tf_op jit(solution)/shard_map/transpose(jvp())/while/body/jit(dynamic_update_index_in_dim)/dynamic_update_slice | solution.py:86
  1679.3 12.8 fusion.318
  1740.2 35.8 %dynamic_update_slice.80 = f32[8,256,24,64]{1,0,3,2:T(8,128)} dynamic-update-slice(f32[8,256,24,64]{1,0,3,2:T(8,128)} %get-tuple-element.1511, f32[1,256,24,64]{1,0,3,2:T(1,128)S(1)} %copy.401, s32[]{:T(128)S(6)} %sub.534, s32[]{:T(128)} %constant.175.clone.1..sunk.2, s32[]{:T(128)} %constant.175.clone.1..sunk.2, s32[]{:T(128)} %constant.175.clone.1..sunk.2) | dynamic-update-slice | bytes 3145732 | tf_op jit(solution)/shard_map/transpose(jvp())/while/body/jit(dynamic_update_index_in_dim)/dynamic_update_slice | solution.py:86
  1794.4 12.8 fusion.318
  1855.4 35.8 %dynamic_update_slice.80 = f32[8,256,24,64]{1,0,3,2:T(8,128)} dynamic-update-slice(f32[8,256,24,64]{1,0,3,2:T(8,128)} %get-tuple-element.1511, f32[1,256,24,64]{1,0,3,2:T(1,128)S(1)} %copy.401, s32[]{:T(128)S(6)} %sub.534, s32[]{:T(128)} %constant.175.clone.1..sunk.2, s32[]{:T(128)} %constant.175.clone.1..sunk.2, s32[]{:T(128)} %constant.175.clone.1..sunk.2) | dynamic-update-slice | bytes 3145732 | tf_op jit(solution)/shard_map/transpose(jvp())/while/body/jit(dynamic_update_index_in_dim)/dynamic_update_slice | solution.py:86
  1909.6 12.8 fusion.318
  1970.6 35.8 %dynamic_update_slice.80 = f32[8,256,24,64]{1,0,3,2:T(8,128)} dynamic-update-slice(f32[8,256,24,64]{1,0,3,2:T(8,128)} %get-tuple-element.1511, f32[1,256,24,64]{1,0,3,2:T(1,128)S(1)} %copy.401, s32[]{:T(128)S(6)} %sub.534, s32[]{:T(128)} %constant.175.clone.1..sunk.2, s32[]{:T(128)} %constant.175.clone.1..sunk.2, s32[]{:T(128)} %constant.175.clone.1..sunk.2) | dynamic-update-slice | bytes 3145732 | tf_op jit(solution)/shard_map/transpose(jvp())/while/body/jit(dynamic_update_index_in_dim)/dynamic_update_slice | solution.py:86
  2024.8 12.8 fusion.318
  2085.8 35.8 %dynamic_update_slice.80 = f32[8,256,24,64]{1,0,3,2:T(8,128)} dynamic-update-slice(f32[8,256,24,64]{1,0,3,2:T(8,128)} %get-tuple-element.1511, f32[1,256,24,64]{1,0,3,2:T(1,128)S(1)} %copy.401, s32[]{:T(128)S(6)} %sub.534, s32[]{:T(128)} %constant.175.clone.1..sunk.2, s32[]{:T(128)} %constant.175.clone.1..sunk.2, s32[]{:T(128)} %constant.175.clone.1..sunk.2) | dynamic-update-slice | bytes 3145732 | tf_op jit(solution)/shard_map/transpose(jvp())/while/body/jit(dynamic_update_index_in_dim)/dynamic_update_slice | solution.py:86
  2140.0 12.8 fusion.318
  2200.9 35.8 %dynamic_update_slice.80 = f32[8,256,24,64]{1,0,3,2:T(8,128)} dynamic-update-slice(f32[8,256,24,64]{1,0,3,2:T(8,128)} %get-tuple-element.1511, f32[1,256,24,64]{1,0,3,2:T(1,128)S(1)} %copy.401, s32[]{:T(128)S(6)} %sub.534, s32[]{:T(128)} %constant.175.clone.1..sunk.2, s32[]{:T(128)} %constant.175.clone.1..sunk.2, s32[]{:T(128)} %constant.175.clone.1..sunk.2) | dynamic-update-slice | bytes 3145732 | tf_op jit(solution)/shard_map/transpose(jvp())/while/body/jit(dynamic_update_index_in_dim)/dynamic_update_slice | solution.py:86
  2255.1 12.8 fusion.318
  2316.1 35.8 %dynamic_update_slice.80 = f32[8,256,24,64]{1,0,3,2:T(8,128)} dynamic-update-slice(f32[8,256,24,64]{1,0,3,2:T(8,128)} %get-tuple-element.1511, f32[1,256,24,64]{1,0,3,2:T(1,128)S(1)} %copy.401, s32[]{:T(128)S(6)} %sub.534, s32[]{:T(128)} %constant.175.clone.1..sunk.2, s32[]{:T(128)} %constant.175.clone.1..sunk.2, s32[]{:T(128)} %constant.175.clone.1..sunk.2) | dynamic-update-slice | bytes 3145732 | tf_op jit(solution)/shard_map/transpose(jvp())/while/body/jit(dynamic_update_index_in_dim)/dynamic_update_slice | solution.py:86
  2361.8 15.4 copy.318
  2377.2 14.1 multiply_add_fusion.2
  2392.0 25.9 multiply_reduce_fusion.7
  2418.0 26.4 multiply_reduce_fusion.6
  2444.5 14.5 slice_multiply_fusion
  2459.0 14.6 slice_multiply_fusion.1
  2475.4 14.9 slice_multiply_fusion.2
  2490.3 30.9 %fusion.190 = (f32[1792]{0:T(1024)S(1)}, f32[1792]{0:T(1024)S(1)}, f32[2048,1792]{0,1:T(8,128)}) fusion(f32[2048,1792]{0,1:T(8,128)} %get-tuple-element.1058, f32[2048,3352]{0,1:T(8,128)} %fusion.173, f32[1792]{0:T(1024)S(1)} %copy-done.26, f32[2047,1792]{0,1:T(8,128)} %slice_multiply_fusion, f32[2046,1792]{0,1:T(8,128)} %slice_multiply_fusion.1, ...), kind=kLoop, calls=%fused_computation.315 | loop fusion | flops 25686528 | bytes 88058880 | tf_op jit(solution)/shard_map/transpose(jvp())/reduce_sum | solution.py:66
  2521.3 22.9 fusion.171
  2545.9 19.3 fusion.152
  2565.2 38.0 %all-reduce.29 = (f32[1792,4]{0,1:T(4,128)S(1)}, f32[1792]{0:T(1024)S(1)}, f32[768]{0:T(1024)S(1)}, f32[1536]{0:T(1024)S(1)}, f32[3,24]{1,0:T(4,128)}) all-reduce(f32[1792,4]{0,1:T(4,128)S(1)} %pad_add_fusion, f32[1792]{0:T(1024)S(1)} %get-tuple-element.964, ...), channel_id=4, replica_groups=mesh['dev'=32] {'dev'}, use_global_device_ids=true, to_apply=%region_34.35.clone | all-reduce | flops 11336 | bytes 90688
  2623.1 102.3 %reduce-scatter.8.cloned.1.call-done = f32[24,3352]{1,0:T(8,128)} async-done(((f32[768,3352]{1,0:T(8,128)}), f32[24,3352]{1,0:T(8,128)}) %reduce-scatter.8.cloned.1.call-update) | async-done | bytes 321808
  (1107 shorter events, 1053.8 us)
Async XLA Ops:
  7.2 95.7 %all-gather.4.cloned.1.call-start = ((), (), s32[]{:S(2)}) async-start(), calls=%async_computation.2 | async-start | bytes 5474304 | tf_op jit(solution)/shard_map/all_gather | solution.py:110
  7.9 802.2 %all-gather.6.cloned.1.call-start = ((), (), s32[]{:S(2)}) async-start(), calls=%async_computation.3 | async-start | bytes 2433024 | tf_op jit(solution)/shard_map/all_gather | solution.py:111
  8.7 2614.4 %reduce-scatter.6.cloned.1.call-start = ((), (), s32[]{:S(2)}) async-start(), calls=%async_computation.4 | async-start | bytes 4866048 | tf_op jit(solution)/shard_map/reduce_scatter | solution.py:159
  9.6 205.1 %copy-start.54 = (f32[24]{0:T(128)}, f32[24]{0:T(128)S(1)}, u32[]{:S(2)}) copy-start(f32[24]{0:T(128)S(1)} %get-tuple-element.1107) | copy-start | bytes 292
  12.3 149.4 %copy-start.27 = (f32[2048]{0:T(1024)}, f32[2048]{0:T(1024)S(1)}, u32[]{:S(2)}) copy-start(f32[2048]{0:T(1024)S(1)} %get-tuple-element.1103) | copy-start | bytes 24580
  12.3 149.4 %copy-start.29 = (f32[2048]{0:T(1024)}, f32[2048]{0:T(1024)S(1)}, u32[]{:S(2)}) copy-start(f32[2048]{0:T(1024)S(1)} %get-tuple-element.1104) | copy-start | bytes 24580
  12.3 149.3 %copy-start.31 = (f32[2048]{0:T(1024)}, f32[2048]{0:T(1024)S(1)}, u32[]{:S(2)}) copy-start(f32[2048]{0:T(1024)S(1)} %get-tuple-element.1105) | copy-start | bytes 24580
  57.2 64.8 %copy-start.49 = (f32[768]{0:T(1024)}, f32[768]{0:T(1024)S(1)}, u32[]{:S(2)}) copy-start(f32[768]{0:T(1024)S(1)} %convert_element_type.220) | copy-start | bytes 9220
  60.5 61.5 %copy-start.43 = (f32[2048]{0:T(1024)}, f32[2048]{0:T(1024)S(1)}, u32[]{:S(2)}) copy-start(f32[2048]{0:T(1024)S(1)} %fusion.184) | copy-start | bytes 24580
  101.5 60.2 %copy-start.25 = (f32[1792]{0:T(1024)}, f32[1792]{0:T(1024)S(1)}, u32[]{:S(2)}) copy-start(f32[1792]{0:T(1024)S(1)} %get-tuple-element.968) | copy-start | bytes 21508
  101.5 60.2 %copy-start.35 = (f32[1792]{0:T(1024)}, f32[1792]{0:T(1024)S(1)}, u32[]{:S(2)}) copy-start(f32[1792]{0:T(1024)S(1)} %get-tuple-element.969) | copy-start | bytes 21508
  101.5 60.2 %copy-start.37 = (f32[1792]{0:T(1024)}, f32[1792]{0:T(1024)S(1)}, u32[]{:S(2)}) copy-start(f32[1792]{0:T(1024)S(1)} %get-tuple-element.970) | copy-start | bytes 21508
  101.5 60.2 %copy-start.39 = (f32[1792]{0:T(1024)}, f32[1792]{0:T(1024)S(1)}, u32[]{:S(2)}) copy-start(f32[1792]{0:T(1024)S(1)} %get-tuple-element.971) | copy-start | bytes 21508
  784.1 18.8 copy-start.20
  784.1 18.8 copy-start.45
  784.2 18.8 copy-start.56
  1508.2 37.5 %copy-start.21 = (f32[1,256,24]{1,2,0:T(8,128)S(1)}, f32[1,256,24]{1,2,0:T(8,128)}, u32[]{:S(2)}) copy-start(f32[1,256,24]{1,2,0:T(8,128)} %get-tuple-element.1405) | copy-start | bytes 73732 | tf_op jit(solution)/shard_map/transpose(jvp())/while
  1508.2 39.2 %copy-start.13 = (f32[8,256,128]{2,1,0:T(8,128)S(1)}, f32[8,256,128]{2,1,0:T(8,128)}, u32[]{:S(2)}) copy-start(f32[8,256,128]{2,1,0:T(8,128)} %copy-done.12) | copy-start | bytes 3145732 | tf_op jit(solution)/shard_map/transpose(jvp())/while
  1508.2 39.2 %copy-start.42 = (f32[24]{0:T(128)S(1)}, f32[24]{0:T(128)}, u32[]{:S(2)}) copy-start(f32[24]{0:T(128)} %get-tuple-element.1581) | copy-start | bytes 292 | tf_op jit(solution)/shard_map/transpose(jvp())/while
  1508.2 39.2 %copy-start.59 = (f32[8]{0:T(128)S(1)}, f32[8]{0:T(128)}, u32[]{:S(2)}) copy-start(f32[8]{0:T(128)} %copy-done.58) | copy-start | bytes 100 | tf_op jit(solution)/shard_map/transpose(jvp())/while
  1623.4 37.5 %copy-start.21 = (f32[1,256,24]{1,2,0:T(8,128)S(1)}, f32[1,256,24]{1,2,0:T(8,128)}, u32[]{:S(2)}) copy-start(f32[1,256,24]{1,2,0:T(8,128)} %get-tuple-element.1405) | copy-start | bytes 73732 | tf_op jit(solution)/shard_map/transpose(jvp())/while
  1623.4 39.2 %copy-start.13 = (f32[8,256,128]{2,1,0:T(8,128)S(1)}, f32[8,256,128]{2,1,0:T(8,128)}, u32[]{:S(2)}) copy-start(f32[8,256,128]{2,1,0:T(8,128)} %copy-done.12) | copy-start | bytes 3145732 | tf_op jit(solution)/shard_map/transpose(jvp())/while
  1623.4 39.2 %copy-start.42 = (f32[24]{0:T(128)S(1)}, f32[24]{0:T(128)}, u32[]{:S(2)}) copy-start(f32[24]{0:T(128)} %get-tuple-element.1581) | copy-start | bytes 292 | tf_op jit(solution)/shard_map/transpose(jvp())/while
  1623.4 39.2 %copy-start.59 = (f32[8]{0:T(128)S(1)}, f32[8]{0:T(128)}, u32[]{:S(2)}) copy-start(f32[8]{0:T(128)} %copy-done.58) | copy-start | bytes 100 | tf_op jit(solution)/shard_map/transpose(jvp())/while
  1704.2 17.6 copy-start.4
  1738.5 37.5 %copy-start.21 = (f32[1,256,24]{1,2,0:T(8,128)S(1)}, f32[1,256,24]{1,2,0:T(8,128)}, u32[]{:S(2)}) copy-start(f32[1,256,24]{1,2,0:T(8,128)} %get-tuple-element.1405) | copy-start | bytes 73732 | tf_op jit(solution)/shard_map/transpose(jvp())/while
  1738.5 39.2 %copy-start.13 = (f32[8,256,128]{2,1,0:T(8,128)S(1)}, f32[8,256,128]{2,1,0:T(8,128)}, u32[]{:S(2)}) copy-start(f32[8,256,128]{2,1,0:T(8,128)} %copy-done.12) | copy-start | bytes 3145732 | tf_op jit(solution)/shard_map/transpose(jvp())/while
  1738.5 39.2 %copy-start.42 = (f32[24]{0:T(128)S(1)}, f32[24]{0:T(128)}, u32[]{:S(2)}) copy-start(f32[24]{0:T(128)} %get-tuple-element.1581) | copy-start | bytes 292 | tf_op jit(solution)/shard_map/transpose(jvp())/while
  1738.6 39.2 %copy-start.59 = (f32[8]{0:T(128)S(1)}, f32[8]{0:T(128)}, u32[]{:S(2)}) copy-start(f32[8]{0:T(128)} %copy-done.58) | copy-start | bytes 100 | tf_op jit(solution)/shard_map/transpose(jvp())/while
  1819.3 17.6 copy-start.4
  1853.7 37.5 %copy-start.21 = (f32[1,256,24]{1,2,0:T(8,128)S(1)}, f32[1,256,24]{1,2,0:T(8,128)}, u32[]{:S(2)}) copy-start(f32[1,256,24]{1,2,0:T(8,128)} %get-tuple-element.1405) | copy-start | bytes 73732 | tf_op jit(solution)/shard_map/transpose(jvp())/while
  1853.7 39.2 %copy-start.13 = (f32[8,256,128]{2,1,0:T(8,128)S(1)}, f32[8,256,128]{2,1,0:T(8,128)}, u32[]{:S(2)}) copy-start(f32[8,256,128]{2,1,0:T(8,128)} %copy-done.12) | copy-start | bytes 3145732 | tf_op jit(solution)/shard_map/transpose(jvp())/while
  1853.7 39.2 %copy-start.42 = (f32[24]{0:T(128)S(1)}, f32[24]{0:T(128)}, u32[]{:S(2)}) copy-start(f32[24]{0:T(128)} %get-tuple-element.1581) | copy-start | bytes 292 | tf_op jit(solution)/shard_map/transpose(jvp())/while
  1853.7 39.2 %copy-start.59 = (f32[8]{0:T(128)S(1)}, f32[8]{0:T(128)}, u32[]{:S(2)}) copy-start(f32[8]{0:T(128)} %copy-done.58) | copy-start | bytes 100 | tf_op jit(solution)/shard_map/transpose(jvp())/while
  1934.5 17.6 copy-start.4
  1968.9 37.5 %copy-start.21 = (f32[1,256,24]{1,2,0:T(8,128)S(1)}, f32[1,256,24]{1,2,0:T(8,128)}, u32[]{:S(2)}) copy-start(f32[1,256,24]{1,2,0:T(8,128)} %get-tuple-element.1405) | copy-start | bytes 73732 | tf_op jit(solution)/shard_map/transpose(jvp())/while
  1968.9 39.2 %copy-start.13 = (f32[8,256,128]{2,1,0:T(8,128)S(1)}, f32[8,256,128]{2,1,0:T(8,128)}, u32[]{:S(2)}) copy-start(f32[8,256,128]{2,1,0:T(8,128)} %copy-done.12) | copy-start | bytes 3145732 | tf_op jit(solution)/shard_map/transpose(jvp())/while
  1968.9 39.2 %copy-start.42 = (f32[24]{0:T(128)S(1)}, f32[24]{0:T(128)}, u32[]{:S(2)}) copy-start(f32[24]{0:T(128)} %get-tuple-element.1581) | copy-start | bytes 292 | tf_op jit(solution)/shard_map/transpose(jvp())/while
  1968.9 39.2 %copy-start.59 = (f32[8]{0:T(128)S(1)}, f32[8]{0:T(128)}, u32[]{:S(2)}) copy-start(f32[8]{0:T(128)} %copy-done.58) | copy-start | bytes 100 | tf_op jit(solution)/shard_map/transpose(jvp())/while
  2049.7 17.6 copy-start.4
  2084.1 37.5 %copy-start.21 = (f32[1,256,24]{1,2,0:T(8,128)S(1)}, f32[1,256,24]{1,2,0:T(8,128)}, u32[]{:S(2)}) copy-start(f32[1,256,24]{1,2,0:T(8,128)} %get-tuple-element.1405) | copy-start | bytes 73732 | tf_op jit(solution)/shard_map/transpose(jvp())/while
  2084.1 39.2 %copy-start.13 = (f32[8,256,128]{2,1,0:T(8,128)S(1)}, f32[8,256,128]{2,1,0:T(8,128)}, u32[]{:S(2)}) copy-start(f32[8,256,128]{2,1,0:T(8,128)} %copy-done.12) | copy-start | bytes 3145732 | tf_op jit(solution)/shard_map/transpose(jvp())/while
  2084.1 39.2 %copy-start.42 = (f32[24]{0:T(128)S(1)}, f32[24]{0:T(128)}, u32[]{:S(2)}) copy-start(f32[24]{0:T(128)} %get-tuple-element.1581) | copy-start | bytes 292 | tf_op jit(solution)/shard_map/transpose(jvp())/while
  2084.1 39.2 %copy-start.59 = (f32[8]{0:T(128)S(1)}, f32[8]{0:T(128)}, u32[]{:S(2)}) copy-start(f32[8]{0:T(128)} %copy-done.58) | copy-start | bytes 100 | tf_op jit(solution)/shard_map/transpose(jvp())/while
  2164.9 17.6 copy-start.4
  2199.3 37.5 %copy-start.21 = (f32[1,256,24]{1,2,0:T(8,128)S(1)}, f32[1,256,24]{1,2,0:T(8,128)}, u32[]{:S(2)}) copy-start(f32[1,256,24]{1,2,0:T(8,128)} %get-tuple-element.1405) | copy-start | bytes 73732 | tf_op jit(solution)/shard_map/transpose(jvp())/while
  2199.3 39.2 %copy-start.13 = (f32[8,256,128]{2,1,0:T(8,128)S(1)}, f32[8,256,128]{2,1,0:T(8,128)}, u32[]{:S(2)}) copy-start(f32[8,256,128]{2,1,0:T(8,128)} %copy-done.12) | copy-start | bytes 3145732 | tf_op jit(solution)/shard_map/transpose(jvp())/while
  2199.3 39.2 %copy-start.42 = (f32[24]{0:T(128)S(1)}, f32[24]{0:T(128)}, u32[]{:S(2)}) copy-start(f32[24]{0:T(128)} %get-tuple-element.1581) | copy-start | bytes 292 | tf_op jit(solution)/shard_map/transpose(jvp())/while
  2199.3 39.2 %copy-start.59 = (f32[8]{0:T(128)S(1)}, f32[8]{0:T(128)}, u32[]{:S(2)}) copy-start(f32[8]{0:T(128)} %copy-done.58) | copy-start | bytes 100 | tf_op jit(solution)/shard_map/transpose(jvp())/while
  2314.4 37.5 %copy-start.21 = (f32[1,256,24]{1,2,0:T(8,128)S(1)}, f32[1,256,24]{1,2,0:T(8,128)}, u32[]{:S(2)}) copy-start(f32[1,256,24]{1,2,0:T(8,128)} %get-tuple-element.1405) | copy-start | bytes 73732 | tf_op jit(solution)/shard_map/transpose(jvp())/while
  2314.4 39.2 %copy-start.13 = (f32[8,256,128]{2,1,0:T(8,128)S(1)}, f32[8,256,128]{2,1,0:T(8,128)}, u32[]{:S(2)}) copy-start(f32[8,256,128]{2,1,0:T(8,128)} %copy-done.12) | copy-start | bytes 3145732 | tf_op jit(solution)/shard_map/transpose(jvp())/while
  2314.4 39.2 %copy-start.42 = (f32[24]{0:T(128)S(1)}, f32[24]{0:T(128)}, u32[]{:S(2)}) copy-start(f32[24]{0:T(128)} %get-tuple-element.1581) | copy-start | bytes 292 | tf_op jit(solution)/shard_map/transpose(jvp())/while
  2314.5 39.2 %copy-start.59 = (f32[8]{0:T(128)S(1)}, f32[8]{0:T(128)}, u32[]{:S(2)}) copy-start(f32[8]{0:T(128)} %copy-done.58) | copy-start | bytes 100 | tf_op jit(solution)/shard_map/transpose(jvp())/while
  2392.0 26.0 copy-start.28
  2392.0 26.0 copy-start.30
  2418.0 26.4 copy-start.40
  2473.6 251.8 %reduce-scatter.8.cloned.1.call-start = ((), (), s32[]{:S(2)}) async-start(), calls=%async_computation.5 | async-start | bytes 10948608
  2490.3 30.9 %copy-start.14 = (bf16[2048,768]{1,0:T(8,128)(2,1)S(1)}, bf16[2048,768]{1,0:T(8,128)(2,1)}, u32[]{:S(2)}) copy-start(bf16[2048,768]{1,0:T(8,128)(2,1)} %param.17) | copy-start | bytes 9437188
  2490.3 30.9 %copy-start.44 = (f32[2048]{0:T(1024)S(1)}, f32[2048]{0:T(1024)}, u32[]{:S(2)}) copy-start(f32[2048]{0:T(1024)} %copy-done.43) | copy-start | bytes 24580
  2490.3 30.9 %copy-start.50 = (f32[768]{0:T(1024)S(1)}, f32[768]{0:T(1024)}, u32[]{:S(2)}) copy-start(f32[768]{0:T(1024)} %copy-done.49) | copy-start | bytes 9220
  2545.8 19.4 copy-start.52
  2545.8 59.7 %copy-start.47 = (f32[2048]{0:T(1024)S(1)}, f32[2048]{0:T(1024)}, u32[]{:S(2)}) copy-start(f32[2048]{0:T(1024)} %get-tuple-element.1094) | copy-start | bytes 24580
  2545.9 59.7 %copy-start.34 = (f32[2048]{0:T(1024)S(1)}, f32[2048]{0:T(1024)}, u32[]{:S(2)}) copy-start(f32[2048]{0:T(1024)} %copy-done.33) | copy-start | bytes 24580
  2612.7 112.7 %copy-start.1 = (s32[8]{0:T(128)S(1)}, s32[8]{0:T(128)}, u32[]{:S(2)}) copy-start(s32[8]{0:T(128)} %param.26) | copy-start | bytes 100
  (119 other events, 1281.2 us)
Sparse Core Ops, SparseCore 0:
  10.9 68.4 all-gather.3
  82.3 56.0 all-gather.5
  2473.8 103.0 reduce-scatter.5
  2584.4 140.9 reduce-scatter.7
where the time goes:
time: 2770 us; the launch traced here: 2730 us
  local copies, waits for them, and re-layouts  1270 us (46%)
  matrix products  656 us (24%)
  other arithmetic  535 us (19%)
  blocking collectives  120 us (4%)
  waiting for transfers between devices  104 us (4%)
  loops' own time  31.1 us (1%)
    dynamic_update_slice x64, local copies, waits for them, and re-layouts, middle(): lax.scan(jax.checkpoint(group_mixer(decay_rate)), initial, pieces)  913 us
    dot_general x32, matrix products, advance(): jnp.einsum('hts,shp->thp', mixing, x_heads, precision=lax.Precision.HIGHEST)  304 us
    dot_general x32, matrix products, advance(): jnp.einsum('sn,shp->hnp', b_rows, weighted, precision=lax.Precision.HIGHEST)  114 us
    convert_element_type x57, other arithmetic, rounded(): value.astype(jnp.bfloat16)  110 us
    unnamed x109, local copies, waits for them, and re-layouts  104 us
    unnamed x5, waiting for transfers between devices  104 us
    another operation x120, other arithmetic  87.5 us
    unnamed x2, blocking collectives  80.3 us
  transfers between devices with their start and end apart: 4, of which 1 were waited for; matrix products, arithmetic and copies ran while one was open for 30% of the time, Pallas kernels for 0%

commit v1 on v0

v1 whole, which is shorter than its diff:
```python
import jax
import jax.numpy as jnp
from jax import lax
from jax.experimental import pallas as pl
from jax.experimental.pallas import tpu as pltpu
from jax.sharding import PartitionSpec as P

HEADS = 24
HEAD_DIM = 64
STATE = 128
KERNEL = 4
GROUP = 256
INNER = 1536
CONV_CH = 1792
D = 768
PROJ = 3352
PAIR = 2 * GROUP
LANES = 128
CHUNKS = INNER // LANES
EPSILON = 1e-05
LOG2E = 1.4426950408889634
F32 = jnp.float32
BF16 = jnp.bfloat16


def mm(left, right, dims=((1,), (0,))):
    return lax.dot_general(left, right, (dims, ((), ())), preferred_element_type=F32)


def exact(left, right):
    return jnp.dot(left, right, precision=lax.Precision.HIGHEST, preferred_element_type=F32)


NT = ((1,), (1,))
TN = ((0,), (0,))


def pair_kernel(
    len_ref, first_ref, proj_ref, raw_ref, tok_ref, cot_ref, outw_ref, cw_ref, cb_ref, gg_ref, heads_ref, skip_ref,
    blk_ref, gn_ref, dproj_ref, dcw_ref, dcb_ref, dgg_ref, dskip_ref, dhead_ref,
    dg_s, y_s, m_s, x_s, b_s, c_s, start_s, s_s, ds_s, db_s, dc_s, at_s, run_s, dt_s, da_s, ddt_s, tot_s,
):
    pair = pl.program_id(0)
    cont = (1 - first_ref[2 * pair + 1]).astype(F32)
    row = lax.broadcasted_iota(jnp.int32, (PAIR, LANES), 0)
    lane = lax.broadcasted_iota(jnp.int32, (PAIR, LANES), 1)
    low_half = lane < HEAD_DIM
    low_g = low_half[:GROUP]
    place = jnp.where(row >= GROUP, row - GROUP, row)
    open_row = jnp.where(row >= GROUP, cont, 0.0)
    tri_t = lax.broadcasted_iota(jnp.int32, (GROUP, GROUP), 0)
    tri_s = lax.broadcasted_iota(jnp.int32, (GROUP, GROUP), 1)
    causal = tri_s <= tri_t

    @pl.when(pair == 0)
    def _():
        dcw_ref[...] = jnp.zeros_like(dcw_ref)
        dcb_ref[...] = jnp.zeros_like(dcb_ref)
        dgg_ref[...] = jnp.zeros_like(dgg_ref)
        dskip_ref[...] = jnp.zeros_like(dskip_ref)
        dhead_ref[...] = jnp.zeros_like(dhead_ref)

    def keep(lag):
        return jnp.where(place >= lag, 1.0, open_row)

    row1 = lax.broadcasted_iota(jnp.int32, (PAIR, 1), 0)
    limit = jnp.where(row1 >= GROUP, len_ref[2 * pair + 1], len_ref[2 * pair])
    live = jnp.where(jnp.where(row1 >= GROUP, row1 - GROUP, row1) < limit, 1.0, 0.0)

    picked = (cot_ref[...].astype(F32) * live).astype(BF16)
    for piece in range(4):
        part = pl.ds(piece * 384, 384)
        dg_s[:, part] = mm(picked, outw_ref[part, :], NT)

    biased = raw_ref[...] + heads_ref[2:3, :]
    small = jnp.exp(-jnp.abs(biased))
    step = jnp.maximum(biased, 0.0) + jnp.where(small < 1e-3, small * (1.0 - 0.5 * small), jnp.log(1.0 + small))
    rate = -jnp.exp(heads_ref[0:1, :])
    log_decay = step * rate
    lower = jnp.where(causal, 1.0, 0.0)
    upper = jnp.where(tri_s >= tri_t, 1.0, 0.0)
    for g in range(2):
        rows = slice(g * GROUP, (g + 1) * GROUP)
        run_s[rows, :] = exact(lower, log_decay[rows]) * LOG2E
    dt_s[...] = step
    at_s[...] = run_s[...].T

    def taps(columns):
        return cw_ref[:, columns], cb_ref[:, columns]

    def conv(j):
        cin = proj_ref[:, pl.ds(pl.multiple_of(INNER + j * LANES, LANES), LANES)]
        columns = pl.ds(pl.multiple_of(j * LANES, LANES), LANES)
        weight, bias = taps(columns)
        mixed = bias + cin * weight[KERNEL - 1 : KERNEL]
        for lag in range(1, KERNEL):
            mixed = mixed + weight[KERNEL - 1 - lag : KERNEL - lag] * (pltpu.roll(cin, lag, 0) * keep(lag))
        m_s[:, columns] = mixed
        return (mixed / (1.0 + jnp.exp(-mixed))).astype(BF16)

    def conv_back(j, grad):
        columns = pl.ds(pl.multiple_of(j * LANES, LANES), LANES)
        place_in = pl.ds(pl.multiple_of(INNER + j * LANES, LANES), LANES)
        weight, _ = taps(columns)
        mixed = m_s[:, columns]
        cin = proj_ref[:, place_in]
        sig = 1.0 / (1.0 + jnp.exp(-mixed))
        dm = grad * (sig * (1.0 + mixed * (1.0 - sig)))
        dcb_ref[:, columns] += jnp.sum(dm, axis=0, keepdims=True)
        total = dm * weight[KERNEL - 1 : KERNEL]
        dws = [jnp.sum(dm * cin, axis=0, keepdims=True)]
        for lag in range(1, KERNEL):
            kept = dm * keep(lag)
            dws.append(jnp.sum(kept * pltpu.roll(cin, lag, 0), axis=0, keepdims=True))
            total = total + pltpu.roll(kept, PAIR - lag, 0) * weight[KERNEL - 1 - lag : KERNEL - lag]
        dcw_ref[:, columns] += jnp.concatenate(dws[::-1], axis=0)
        dproj_ref[:, place_in] = total.astype(BF16)

    b_s[...] = conv(CHUNKS)
    c_s[...] = conv(CHUNKS + 1)
    for g in range(2):
        rows = slice(g * GROUP, (g + 1) * GROUP)
        s_s[g] = jnp.where(causal, mm(c_s[rows, :], b_s[rows, :], NT), 0.0)
        ds_s[g] = jnp.zeros((GROUP, GROUP), F32)
    db_s[...] = jnp.zeros_like(db_s)
    dc_s[...] = jnp.zeros_like(dc_s)
    da_s[...] = jnp.zeros_like(da_s)
    ddt_s[...] = jnp.zeros_like(ddt_s)
    tot_s[...] = jnp.zeros_like(tot_s)

    def column(table, h):
        return jnp.sum(jnp.where(lane == h, table, 0.0), axis=1, keepdims=True)

    def head_columns(hp):
        run, dt = run_s[...], dt_s[...]
        runs = (column(run, 2 * hp), column(run, 2 * hp + 1))
        dts = jnp.where(low_half, column(dt, 2 * hp), column(dt, 2 * hp + 1))
        return runs, jnp.where(low_half, runs[0], runs[1]), dts

    def decay(runs, hp, g, k):
        rows = slice(g * GROUP, (g + 1) * GROUP)
        across = at_s[pl.ds(2 * hp + k, 1), rows]
        return jnp.exp2(jnp.minimum(runs[k][rows] - across, 0.0))

    def to_end(wide):
        return jnp.exp2(wide[GROUP - 1 : GROUP] - wide[:GROUP])

    def forward(hp, sums):
        square, cross = sums
        columns = pl.ds(pl.multiple_of(hp * LANES, LANES), LANES)
        x_low = conv(hp)
        x_s[:, columns] = x_low
        x = x_low.astype(F32)
        runs, wide, dts = head_columns(hp)
        xdt = (x * dts).astype(BF16)
        weighted = (x[:GROUP] * (to_end(wide) * dts[:GROUP])).astype(BF16)
        start = (mm(b_s[:GROUP, :], weighted, TN) * cont).astype(BF16)
        start_s[:, columns] = start
        inner = []
        for g in range(2):
            rows = slice(g * GROUP, (g + 1) * GROUP)
            halves = [mm((s_s[g] * decay(runs, hp, g, k)).astype(BF16), xdt[rows]) for k in range(2)]
            inner.append(jnp.where(low_g, halves[0], halves[1]))
        inner[1] = inner[1] + jnp.exp2(wide[GROUP:]) * mm(c_s[GROUP:, :], start)
        y = jnp.concatenate(inner, axis=0)
        y_s[:, columns] = y
        gate = proj_ref[:, columns]
        gated = (y + skip_ref[:, columns] * x) * (gate / (1.0 + jnp.exp(-gate)))
        return (square + gated * gated, cross + dg_s[:, columns] * gg_ref[:, columns] * gated)

    zero = jnp.zeros((PAIR, LANES), F32)
    square, cross = lax.fori_loop(0, CHUNKS, forward, (zero, zero))
    scale = lax.rsqrt(jnp.sum(square, axis=1, keepdims=True) * (1.0 / INNER) + EPSILON)
    pull = scale * scale * scale * (jnp.sum(cross, axis=1, keepdims=True) * (1.0 / INNER))

    def put(h, value):
        return jnp.where(lane[: value.shape[0]] == h, value, 0.0)

    def head_sums(hp, value):
        first = jnp.sum(jnp.where(low_half[: value.shape[0]], value, 0.0), axis=1, keepdims=True)
        second = jnp.sum(jnp.where(low_half[: value.shape[0]], 0.0, value), axis=1, keepdims=True)
        return put(2 * hp, first) + put(2 * hp + 1, second)

    def backward(hp, carry):
        columns = pl.ds(pl.multiple_of(hp * LANES, LANES), LANES)
        x = x_s[:, columns].astype(F32)
        y = y_s[:, columns]
        skip = skip_ref[:, columns]
        mixer = y + skip * x
        gate = proj_ref[:, columns]
        sig = 1.0 / (1.0 + jnp.exp(-gate))
        act = gate * sig
        gated = mixer * act
        gain = gg_ref[:, columns]
        dgn = dg_s[:, columns]
        unit = gated * scale
        gn_ref[:, columns] = (unit * gain).astype(BF16)
        dgg_ref[:, columns] += jnp.sum(dgn * unit, axis=0, keepdims=True)
        dgated = dgn * gain * scale - gated * pull
        dproj_ref[:, columns] = (dgated * mixer * (sig * (1.0 + gate * (1.0 - sig)))).astype(BF16)
        dy = dgated * act
        dskip_ref[:, columns] += jnp.sum(dy * x, axis=0, keepdims=True)
        dy_low = dy.astype(BF16)
        dyr = dy_low.astype(F32)
        runs, wide, dts = head_columns(hp)
        xdt = (x * dts).astype(BF16)
        dxdt = []
        for g in range(2):
            rows = slice(g * GROUP, (g + 1) * GROUP)
            parts = []
            extra = jnp.zeros((GROUP, GROUP), F32)
            dy_g = dy_low[rows]
            for k in range(2):
                fade = decay(runs, hp, g, k)
                parts.append(mm((s_s[g] * fade).astype(BF16), dy_g, TN))
                mine = jnp.where(low_g if k == 0 else ~low_g, dyr[rows], 0.0).astype(BF16)
                extra = extra + mm(mine, xdt[rows], NT) * fade
            ds_s[g] += extra
            dxdt.append(jnp.where(low_g, parts[0], parts[1]))
        dxdt = jnp.concatenate(dxdt, axis=0)
        start = start_s[:, columns]
        lifted = (dyr[GROUP:] * jnp.exp2(wide[GROUP:])).astype(BF16)
        dc_s[GROUP:, :] += mm(lifted, start, NT)
        dstate = (mm(c_s[GROUP:, :], lifted, TN) * cont).astype(BF16)
        fade_end = to_end(wide)
        weight_end = fade_end * dts[:GROUP]
        weighted = (x[:GROUP] * weight_end).astype(BF16)
        db_s[:GROUP, :] += mm(weighted, dstate, NT)
        dweighted = mm(b_s[:GROUP, :], dstate)
        through = x[:GROUP] * dweighted
        spent = through * weight_end
        da = dyr * y - xdt.astype(F32) * dxdt
        ddt = x * dxdt
        da = jnp.concatenate([da[:GROUP] - spent, da[GROUP:]], axis=0)
        ddt = jnp.concatenate([ddt[:GROUP] + through * fade_end, ddt[GROUP:]], axis=0)
        da_s[...] += head_sums(hp, da)
        ddt_s[...] += head_sums(hp, ddt)
        tot_s[...] += head_sums(hp, jnp.broadcast_to(jnp.sum(spent, axis=0, keepdims=True), (8, LANES)))
        dx = dy * skip + dxdt * dts
        dx = jnp.concatenate([dx[:GROUP] + dweighted * weight_end, dx[GROUP:]], axis=0)
        conv_back(hp, dx)
        return carry

    lax.fori_loop(0, CHUNKS, backward, 0)

    for g in range(2):
        rows = slice(g * GROUP, (g + 1) * GROUP)
        dscore = jnp.where(causal, ds_s[g], 0.0).astype(BF16)
        dc_s[rows, :] += mm(dscore, b_s[rows, :])
        db_s[rows, :] += mm(dscore, c_s[rows, :], TN)
    conv_back(CHUNKS, db_s[...])
    conv_back(CHUNKS + 1, dc_s[...])

    dlog = []
    for g in range(2):
        rows = slice(g * GROUP, (g + 1) * GROUP)
        part = exact(upper, da_s[rows, :])
        dlog.append(part + tot_s[0:1, :] if g == 0 else part)
    dlog = jnp.concatenate(dlog, axis=0)
    step = dt_s[...]
    dstep = ddt_s[...] + dlog * rate
    draw = dstep / (1.0 + jnp.exp(-biased))
    dproj_ref[:, PROJ - HEADS : PROJ] = draw[:, :HEADS].astype(BF16)
    dhead_ref[0:1, :] += jnp.sum(dlog * step, axis=0, keepdims=True) * rate
    dhead_ref[2:3, :] += jnp.sum(draw, axis=0, keepdims=True)

    branch = mm(gn_ref[...], outw_ref[...])
    blk_ref[...] = (tok_ref[...].astype(F32) + live * branch).astype(BF16)


def run_pairs(lengths, firsts, projected, raw, tokens, cotangent, out_w, cw, cb, gg, heads, skip):
    rows = tokens.shape[0]

    def rowwise(width):
        return pl.BlockSpec((PAIR, width), lambda i: (i, 0))

    smem = pl.BlockSpec(memory_space=pltpu.SMEM)
    whole = pl.BlockSpec(memory_space=pltpu.VMEM)
    shape = jax.ShapeDtypeStruct
    return pl.pallas_call(
        pair_kernel,
        grid=(rows // PAIR,),
        in_specs=[smem, smem, rowwise(PROJ), rowwise(LANES), rowwise(D), rowwise(D)] + [whole] * 6,
        out_specs=[rowwise(D), rowwise(INNER), rowwise(PROJ)] + [whole] * 5,
        out_shape=[
            shape((rows, D), BF16),
            shape((rows, INNER), BF16),
            shape((rows, PROJ), BF16),
            shape((KERNEL, CONV_CH), F32),
            shape((1, CONV_CH), F32),
            shape((1, INNER), F32),
            shape((1, INNER), F32),
            shape((8, LANES), F32),
        ],
        scratch_shapes=[
            pltpu.VMEM((PAIR, INNER), F32),
            pltpu.VMEM((PAIR, INNER), F32),
            pltpu.VMEM((PAIR, CONV_CH), F32),
            pltpu.VMEM((PAIR, INNER), BF16),
            pltpu.VMEM((PAIR, LANES), BF16),
            pltpu.VMEM((PAIR, LANES), BF16),
            pltpu.VMEM((STATE, INNER), BF16),
            pltpu.VMEM((2, GROUP, GROUP), F32),
            pltpu.VMEM((2, GROUP, GROUP), F32),
            pltpu.VMEM((PAIR, LANES), F32),
            pltpu.VMEM((PAIR, LANES), F32),
            pltpu.VMEM((LANES, PAIR), F32),
            pltpu.VMEM((PAIR, LANES), F32),
            pltpu.VMEM((PAIR, LANES), F32),
            pltpu.VMEM((PAIR, LANES), F32),
            pltpu.VMEM((PAIR, LANES), F32),
            pltpu.VMEM((8, LANES), F32),
        ],
        compiler_params=pltpu.CompilerParams(
            dimension_semantics=("arbitrary",), vmem_limit_bytes=60 * 1024 * 1024
        ),
    )(lengths, firsts, projected, raw, tokens, cotangent, out_w, cw, cb, gg, heads, skip)


def body(
    tokens,
    cotangent,
    in_weight,
    out_weight,
    conv_weight,
    conv_bias,
    norm_gain,
    gated_gain,
    head_params,
    group_length,
    group_first,
):
    sizes = (conv_weight.size, conv_bias.size, norm_gain.size, gated_gain.size)
    cuts = (sizes[0], sizes[0] + sizes[1], sizes[0] + sizes[1] + sizes[2])
    packed = jnp.concatenate([conv_weight.reshape(-1), conv_bias, norm_gain, gated_gain])
    packed = lax.all_gather(packed[None], "dev", axis=0, tiled=True).astype(F32)
    conv_w, conv_b, norm_g, gated_g = jnp.split(packed, cuts, axis=1)
    conv_w = conv_w.reshape(CONV_CH, KERNEL).T
    conv_b, norm_g, gated_g = conv_b.reshape(1, -1), norm_g.reshape(1, -1), gated_g.reshape(1, -1)
    in_w = lax.all_gather(in_weight, "dev", axis=0, tiled=True)
    out_w = lax.all_gather(out_weight, "dev", axis=0, tiled=True)
    ndev = packed.shape[0]

    token_float = tokens.astype(F32)
    inv = lax.rsqrt(jnp.mean(token_float * token_float, axis=1, keepdims=True) + EPSILON)
    normed_low = (token_float * inv * norm_g).astype(BF16)
    projected = jnp.dot(normed_low, in_w, preferred_element_type=F32)
    raw = jnp.pad(projected[:, PROJ - HEADS :], ((0, 0), (0, LANES - HEADS)))
    heads = jnp.pad(head_params, ((0, 5), (0, LANES - HEADS)))
    skip = jnp.repeat(head_params[1], HEAD_DIM)[None, :]
    block_out, gnormed_low, grad_proj, dcw, dcb, dgg, dskip, dhead = run_pairs(
        group_length, group_first, projected, raw, tokens, cotangent, out_w, conv_w, conv_b, gated_g, heads, skip
    )

    rows = tokens.shape[0]
    slot_place = jnp.arange(rows, dtype=jnp.int32) % GROUP
    live_mask = (slot_place < jnp.repeat(group_length, GROUP)).astype(BF16)[:, None]
    picked = cotangent * live_mask
    out_grad = jnp.dot(gnormed_low.T, picked, preferred_element_type=F32)
    out_grad = lax.psum_scatter(out_grad, "dev", scatter_dimension=0, tiled=True)
    in_grad = jnp.dot(normed_low.T, grad_proj, preferred_element_type=F32)
    in_grad = lax.psum_scatter(in_grad, "dev", scatter_dimension=0, tiled=True)
    grad_normed = jnp.dot(grad_proj, in_w.T, preferred_element_type=F32)
    unit = token_float * inv
    grad_norm_g = jnp.sum(grad_normed * unit, axis=0)
    scaled = grad_normed * norm_g
    grad_tokens = inv * (scaled - unit * jnp.mean(scaled * unit, axis=1, keepdims=True))
    token_grad = cotangent.astype(F32) + grad_tokens

    small = jnp.concatenate(
        [
            dcw.T.reshape(ndev, -1),
            dcb.reshape(ndev, -1),
            grad_norm_g.reshape(ndev, -1),
            dgg.reshape(ndev, -1),
        ],
        axis=1,
    )
    width = small.shape[1]
    head_part = jnp.stack([dhead[0, :HEADS], jnp.sum(dskip.reshape(HEADS, HEAD_DIM), axis=1), dhead[2, :HEADS]])
    total = lax.psum(jnp.concatenate([small.reshape(-1), head_part.reshape(-1)]), "dev")
    head_total = total[ndev * width :].reshape(3, HEADS)
    mine = lax.dynamic_slice(total, (lax.axis_index("dev") * width,), (width,))
    cw_o, cb_o, ng_o, gg_o = jnp.split(mine, cuts)
    return (
        block_out,
        token_grad,
        in_grad,
        out_grad,
        cw_o.reshape(conv_weight.shape),
        cb_o,
        ng_o,
        gg_o,
        head_total,
    )


def solution(mesh):
    placed = (
        P("dev", None),
        P("dev", None),
        P("dev", None),
        P("dev", None),
        P("dev", None),
        P("dev"),
        P("dev"),
        P("dev"),
        P(),
        P("dev"),
        P("dev"),
    )
    return jax.shard_map(
        body,
        mesh=mesh,
        in_specs=placed,
        out_specs=(
            P("dev", None),
            P("dev", None),
            P("dev", None),
            P("dev", None),
            P("dev", None),
            P("dev"),
            P("dev"),
            P("dev"),
            P(),
        ),
        check_vma=False,
    )
```

time: 2770 us -> 559 us (0.20); the launches traced: 2730 us -> 558 us
  local copies, waits for them, and re-layouts: 1270 us -> 17.2 us
  matrix products: 656 us -> 66.6 us
  other arithmetic: 535 us -> 10.1 us
  Pallas kernels: 0 us -> 148 us
  waiting for transfers between devices: 104 us -> 220 us
  blocking collectives: 120 us -> 82.3 us
  loops' own time: 31.1 us -> 0 us
    dynamic_update_slice x64 -> x0, local copies, waits for them, and re-layouts: 913 us -> none  [middle(): lax.scan(jax.checkpoint(group_mixer(decay_rate)), initial, pieces)]
    dot_general x126 -> x4, matrix products: 607 us -> 66.6 us  [the longest x1 19.9 us: body(): projected = jnp.dot(normed_low, in_w, preferred_element_type=F32)]
    reduce_sum x32 -> x2, other arithmetic: 165 us -> 2.69 us  [the longest x1 2.57 us: body(): jnp.mean(token_float * token_float, axis=1, keepdims=True) + EPSILON]
    pallas_call x0 -> x1, Pallas kernels: none -> 148 us  [run_pairs(): pl.pallas_call(pair_kernel, grid=(rows // PAIR,), in_specs=[smem, smem, r...]
    convert_element_type x63 -> x1, other arithmetic: 111 us -> 0.01 us  [body(): (slot_place < jnp.repeat(group_length, GROUP)).astype(BF16)[:, None]]
    unnamed x109 -> x16, local copies, waits for them, and re-layouts: 104 us -> 2.45 us
    another operation x128 -> x1, other arithmetic: 95.8 us -> 0.01 us  [body(): jnp.stack([dhead[0, :HEADS], jnp.sum(dskip.reshape(HEADS, HEAD_DIM), axis...]
    dynamic_slice x32 -> x1, local copies, waits for them, and re-layouts: 62.4 us -> 0.08 us  [body(): mine = lax.dynamic_slice(total, (lax.axis_index('dev') * width,), (width,))]
  transfers between devices with their start and end apart: 4 -> 4, of which waited for: 1 -> 4; matrix products, arithmetic and copies ran while one was open for 30% -> 15% of each run, Pallas kernels for 0% -> 0%
where the time goes in v1:
time: 559 us; the launch traced here: 558 us
  waiting for transfers between devices  220 us (39%)
  Pallas kernels  148 us (26%)
  blocking collectives  82.3 us (15%)
  matrix products  66.6 us (12%)
  local copies, waits for them, and re-layouts  17.2 us (3%)
  between operations  14 us (3%)
  other arithmetic  10.1 us (2%)
    unnamed x5, waiting for transfers between devices  150 us
    pallas_call x1, Pallas kernels, run_pairs(): pl.pallas_call(pair_kernel, grid=(rows // PAIR,), in_specs=[smem, smem, r...  148 us
    unnamed x1, blocking collectives  42.8 us
    psum x1, blocking collectives, body(): lax.psum(jnp.concatenate([small.reshape(-1), head_part.reshape(-1)]), 'dev')  39.5 us
    all_gather x1, waiting for transfers between devices, body(): out_w = lax.all_gather(out_weight, 'dev', axis=0, tiled=True)  36.8 us
    dot_general x1, matrix products, body(): projected = jnp.dot(normed_low, in_w, preferred_element_type=F32)  19.9 us
    dot_general x1, matrix products, body(): grad_normed = jnp.dot(grad_proj, in_w.T, preferred_element_type=F32)  18.8 us
    dot_general x1, matrix products, body(): in_grad = jnp.dot(normed_low.T, grad_proj, preferred_element_type=F32)  17.9 us
  transfers between devices with their start and end apart: 4, of which 4 were waited for; matrix products, arithmetic and copies ran while one was open for 15% of the time, Pallas kernels for 0%

profile of v1, /device:TPU:0, one launch (start us, length us, event | category | flops | bytes accessed | tf_op | source)
XLA Modules:
  0.0 558.4 jit_solution(357690975247962056)
XLA Ops:
  7.2 0.0 all-gather.4.cloned.1.call-start
  7.2 0.7 all-gather.4.cloned.1.call-update
  7.9 0.0 all-gather.6.cloned.1.call-start
  8.0 0.7 all-gather.6.cloned.1.call-update
  8.7 0.0 reduce-scatter.5.cloned.1.call-start
  8.7 0.8 copy.28
  9.5 0.1 reshape.97
  9.6 0.8 pad_maximum_fusion.3
  10.4 0.3 dynamic-update-slice
  10.6 42.8 %all-reduce.2 = bf16[11264]{0:T(1024)(128)(2,1)S(1)} all-reduce(bf16[11264]{0:T(1024)(128)(2,1)S(1)} %dynamic-update-slice), channel_id=2, replica_groups=mesh['dev'=32] {'dev'}, use_global_device_ids=true, to_apply=%add.2 | all-reduce | flops 11264 | bytes 45056
  53.5 0.1 reshape.112
  53.6 0.1 split.32
  53.6 0.1 split.34
  53.7 0.1 split.35
  53.8 0.1 mul.65
  53.9 0.3 reshape.98
  54.2 0.9 copy.30
  55.1 0.7 reshape.99.cb_ref
  55.8 0.7 reshape.100.gg_ref
  56.4 0.7 slice_bitcast_fusion
  57.1 0.1 broadcast_in_dim.13
  57.2 0.7 broadcast_in_dim_reshape.3.skip_ref
  57.9 1.3 pad.9.heads_ref
  59.2 0.7 broadcast_bitcast_fusion
  59.9 2.6 fusion.10
  62.5 16.8 %all-gather.4.cloned.1.call-done = bf16[768,3352]{1,0:T(8,128)(2,1)} async-done(((bf16[24,3352]{1,0:T(8,128)(2,1)}), bf16[768,3352]{1,0:T(8,128)(2,1)}) %all-gather.4.cloned.1.call-update) | async-done | bytes 5148688 | tf_op jit(solution)/shard_map/all_gather | solution.py:340
  79.3 19.9 %fusion.16.proj_ref = f32[2048,3352]{1,0:T(8,128)} fusion(bf16[768,3352]{1,0:T(8,128)(2,1)} %all-gather.4.cloned.1.call-done, bf16[2048,768]{1,0:T(8,128)(2,1)} %tok_ref.1, f32[768]{0:T(1024)S(1)} %mul.65, f32[2048]{0:T(1024)S(1)} %add_rsqrt_fusion), kind=kOutput, calls=%fused_computation.17 | convolution fusion | flops 10550771712 | bytes 35765248 | tf_op jit(solution)/shard_map/dot_general | solution.py:347
  99.3 1.3 slice.28
  100.6 1.0 pad.8.raw_ref
  101.6 36.8 %all-gather.6.cloned.1.call-done.outw_ref = bf16[1536,768]{1,0:T(8,128)(2,1)} async-done(((bf16[48,768]{1,0:T(8,128)(2,1)}), bf16[1536,768]{1,0:T(8,128)(2,1)}) %all-gather.6.cloned.1.call-update) | async-done | bytes 2359312 | tf_op jit(solution)/shard_map/all_gather | solution.py:341
  138.4 147.9 %shard_map.178 = (bf16[2048,768]{1,0:T(8,128)(2,1)}, bf16[2048,1536]{1,0:T(8,128)(2,1)}, bf16[2048,3352]{1,0:T(8,128)(2,1)}, f32[4,1792]{1,0:T(4,128)}, f32[1,17...) custom-call(s32[8]{0:T(128)} %len_ref.1, s32[8]{0:T(128)} %first_ref.1, ...), custom_call_target="tpu_custom_call" | custom-call | tf_op jit(solution)/shard_map/pallas_call | solution.py:280
  286.3 0.0 copy-start
  286.3 9.9 %fusion.11 = f32[1536,768]{1,0:T(8,128)} fusion(bf16[2048,1536]{1,0:T(8,128)(2,1)} %get-tuple-element.19, bf16[2048,768]{1,0:T(8,128)(2,1)} %cot_ref.1, bf16[2048]{0:T(1024)(128)(2,1)S(1)} %fusion.22), kind=kOutput, calls=%fused_computation.13 | convolution fusion | flops 4833411072 | bytes 14159872 | tf_op jit(solution)/shard_map/dot_general | solution.py:359
  296.2 0.0 reduce-scatter.5.cloned.1.call-update
  296.3 0.0 reduce-scatter.7.cloned.1.call-start
  296.3 0.0 copy-done
  296.3 17.9 %fusion.14 = f32[768,3352]{1,0:T(8,128)} fusion(bf16[2048,3352]{1,0:T(8,128)(2,1)} %get-tuple-element.18, bf16[2048,768]{1,0:T(8,128)(2,1)S(1)} %copy-done, f32[768]{0:T(1024)S(1)} %mul.65, f32[2048]{0:T(1024)S(1)} %add_rsqrt_fusion), kind=kOutput, calls=%fused_computation.16 | convolution fusion | flops 10550771712 | bytes 27184128 | tf_op jit(solution)/shard_map/dot_general | solution.py:361
  314.2 0.0 reduce-scatter.7.cloned.1.call-update
  314.2 0.0 copy-start.1
  314.2 0.0 copy-start.2
  314.3 18.8 %fusion.9 = (f32[768]{0:T(1024)S(1)}, f32[2048]{0:T(1024)S(1)}, f32[2048,768]{1,0:T(8,128)}) fusion(bf16[2048,768]{1,0:T(8,128)(2,1)S(1)} %copy-done, f32[2048]{0:T(1024)S(1)} %add_rsqrt_fusion, f32[768]{0:T(1024)S(1)} %mul.65, bf16[2048,3352]{1,0:T(8,128)(2,1)} %get-tuple-element.18, bf16[768,3352]{1,0:T(8,128)(2,1)} %all-gather.4.cloned.1.call-done), kind=kOutput, calls=%fused_computation.11 | convolution fusion | flops 10555487232 | bytes 28338176 | tf_op jit(solution)/shard_map/dot_general | solution.py:363
  333.1 0.1 reshape.104
  333.2 1.3 copy.32
  334.4 1.5 reshape.102
  336.0 0.1 reshape.103
  336.1 0.0 copy-done.4
  336.1 0.1 reshape.105
  336.2 0.1 pad_maximum_fusion
  336.3 0.1 reshape.106
  336.4 0.1 reshape.107
  336.5 0.1 reduce_sum.39
  336.6 0.8 fusion.23
  337.4 0.1 reshape.108
  337.5 39.5 %psum.7 = f32[11336]{0:T(1024)S(1)} all-reduce(f32[11336]{0:T(1024)S(1)} %pad_maximum_fusion.1), channel_id=1, replica_groups=mesh['dev'=32] {'dev'}, use_global_device_ids=true, to_apply=%region_6.7 | all-reduce | flops 11336 | bytes 90688 | tf_op jit(solution)/shard_map/psum | solution.py:381
  377.0 0.1 dynamic_slice.3
  377.0 0.6 split.29
  377.6 0.6 split.30
  378.2 0.6 split.31
  378.8 0.1 reshape.109
  378.9 0.7 copy.33
  379.5 0.7 reshape.110
  380.2 6.4 %fusion.8 = f32[2048,768]{1,0:T(8,128)} fusion(bf16[2048,768]{1,0:T(8,128)(2,1)S(1)} %copy-done, bf16[2048,768]{1,0:T(8,128)(2,1)} %cot_ref.1, f32[2048,768]{1,0:T(8,128)} %get-tuple-element.47, f32[2048]{0:T(1024)S(1)} %broadcast_multiply_fusion, f32[768]{0:T(1024)S(1)} %mul.65, f32[2048]{0:T(1024)S(1)} %add_rsqrt_fusion), kind=kLoop, calls=%fused_computation.10 | loop fusion | flops 12582912 | bytes 18893824 | tf_op jit(solution)/shard_map/add | solution.py:368
  386.6 16.7 %reduce-scatter.5.cloned.1.call-done = f32[48,768]{1,0:T(8,128)} async-done(((f32[1536,768]{1,0:T(8,128)}), f32[48,768]{1,0:T(8,128)}) %reduce-scatter.5.cloned.1.call-update) | async-done | bytes 147472 | tf_op jit(solution)/shard_map/reduce_scatter | solution.py:360
  403.3 148.5 %reduce-scatter.7.cloned.1.call-done = f32[24,3352]{1,0:T(8,128)} async-done(((f32[768,3352]{1,0:T(8,128)}), f32[24,3352]{1,0:T(8,128)}) %reduce-scatter.7.cloned.1.call-update) | async-done | bytes 321808
  (18 shorter events, 0.1 us)
Async XLA Ops:
  7.2 72.2 %all-gather.4.cloned.1.call-start = ((), (), s32[]{:S(2)}) async-start(), calls=%async_computation.2 | async-start | bytes 5474304 | tf_op jit(solution)/shard_map/all_gather | solution.py:340
  7.9 130.5 %all-gather.6.cloned.1.call-start = ((), (), s32[]{:S(2)}) async-start(), calls=%async_computation.3 | async-start | bytes 2433024 | tf_op jit(solution)/shard_map/all_gather | solution.py:341
  8.7 394.7 %reduce-scatter.5.cloned.1.call-start = ((), (), s32[]{:S(2)}) async-start(), calls=%async_computation.4 | async-start | bytes 4866048 | tf_op jit(solution)/shard_map/reduce_scatter | solution.py:360
  286.3 10.0 %copy-start = (bf16[2048,768]{1,0:T(8,128)(2,1)S(1)}, bf16[2048,768]{1,0:T(8,128)(2,1)}, u32[]{:S(2)}) copy-start(bf16[2048,768]{1,0:T(8,128)(2,1)} %tok_ref.1) | copy-start | bytes 9437188
  296.3 255.6 %reduce-scatter.7.cloned.1.call-start = ((), (), s32[]{:S(2)}) async-start(), calls=%async_computation.5 | async-start | bytes 10948608
  314.2 18.9 %copy-start.1 = (f32[4,1792]{1,0:T(4,128)S(1)}, f32[4,1792]{1,0:T(4,128)}, u32[]{:S(2)}) copy-start(f32[4,1792]{1,0:T(4,128)} %get-tuple-element.20) | copy-start | bytes 86020
  314.2 21.7 %copy-start.2 = (f32[1,1792]{1,0:T(1,128)S(1)}, f32[1,1792]{1,0:T(1,128)}, u32[]{:S(2)}) copy-start(f32[1,1792]{1,0:T(1,128)} %get-tuple-element.21) | copy-start | bytes 21508
  314.2 21.8 %copy-start.4 = (f32[1,1536]{1,0:T(1,128)S(1)}, f32[1,1536]{1,0:T(1,128)}, u32[]{:S(2)}) copy-start(f32[1,1536]{1,0:T(1,128)} %get-tuple-element.22) | copy-start | bytes 18436
  314.3 22.1 %copy-start.3 = (f32[1,1536]{1,0:T(1,128)S(1)}, f32[1,1536]{1,0:T(1,128)}, u32[]{:S(2)}) copy-start(f32[1,1536]{1,0:T(1,128)} %get-tuple-element.24) | copy-start | bytes 18436
Sparse Core Ops, SparseCore 0:
  10.9 68.3 all-gather.3
  82.2 56.1 all-gather.5
  296.4 106.9 reduce-scatter.4
  410.9 140.9 reduce-scatter.6

commit v2 on v1

--- a/solution.py
+++ b/solution.py
@@ -317,6 +317,50 @@
     )(lengths, firsts, projected, raw, tokens, cotangent, out_w, cw, cb, gg, heads, skip)
 
 
+def partners(count, bit):
+    return [(i, i ^ (1 << bit)) for i in range(count)]
+
+
+def own_bit(bit):
+    return lax.rem(lax.div(lax.axis_index("dev"), 1 << bit), 2)
+
+
+def bit_orders(count):
+    bits = list(range(count.bit_length() - 1))
+    swapped = [bits[0], bits[2], bits[1]] + bits[3:] if len(bits) > 2 else bits
+    return bits, swapped
+
+
+def gather_blocks(block, count, order):
+    held = []
+    for bit in order[::-1]:
+        other = lax.ppermute(block, "dev", partners(count, bit))
+        mine = own_bit(bit) == 1
+        axis = sum(1 for done in held if done > bit)
+        block = jnp.stack([jnp.where(mine, other, block), jnp.where(mine, block, other)], axis=axis)
+        held.append(bit)
+    return block.reshape((count,) + block.shape[len(held) :])
+
+
+def scatter_sums(blocks, count, order, sent):
+    left = list(range(count.bit_length() - 1))[::-1]
+    blocks = blocks.reshape((2,) * len(left) + blocks.shape[1:])
+    for bit in order:
+        axis = left.index(bit)
+        mine = own_bit(bit)
+        away = lax.dynamic_index_in_dim(blocks, 1 - mine, axis, keepdims=False).astype(sent)
+        kept = lax.dynamic_index_in_dim(blocks, mine, axis, keepdims=False)
+        blocks = kept + lax.ppermute(away, "dev", partners(count, bit)).astype(F32)
+        left.remove(bit)
+    return blocks
+
+
+def sum_all(value, count):
+    for bit in range(count.bit_length() - 1):
+        value = value + lax.ppermute(value, "dev", partners(count, bit))
+    return value
+
+
 def body(
     tokens,
     cotangent,
@@ -332,14 +376,21 @@
 ):
     sizes = (conv_weight.size, conv_bias.size, norm_gain.size, gated_gain.size)
     cuts = (sizes[0], sizes[0] + sizes[1], sizes[0] + sizes[1] + sizes[2])
+    ndev = lax.axis_size("dev")
+    plain, swapped = bit_orders(ndev)
+    owned, width = in_weight.shape
+    upper = (owned // 3) * 2
     packed = jnp.concatenate([conv_weight.reshape(-1), conv_bias, norm_gain, gated_gain])
-    packed = lax.all_gather(packed[None], "dev", axis=0, tiled=True).astype(F32)
+    extra = -(-packed.size // (owned - upper))
+    packed = jnp.pad(packed, (0, extra * (owned - upper) - packed.size)).reshape(owned - upper, extra)
+    first_rows = gather_blocks(in_weight[:upper], ndev, plain)
+    last_rows = gather_blocks(jnp.concatenate([in_weight[upper:], packed], axis=1), ndev, swapped)
+    out_w = gather_blocks(out_weight, ndev, swapped).reshape(INNER, D)
+    in_w = jnp.concatenate([first_rows, last_rows[:, :, :width]], axis=1).reshape(D, width)
+    packed = last_rows[:, :, width:].reshape(ndev, -1)[:, : cuts[2] + sizes[3]].astype(F32)
     conv_w, conv_b, norm_g, gated_g = jnp.split(packed, cuts, axis=1)
     conv_w = conv_w.reshape(CONV_CH, KERNEL).T
     conv_b, norm_g, gated_g = conv_b.reshape(1, -1), norm_g.reshape(1, -1), gated_g.reshape(1, -1)
-    in_w = lax.all_gather(in_weight, "dev", axis=0, tiled=True)
-    out_w = lax.all_gather(out_weight, "dev", axis=0, tiled=True)
-    ndev = packed.shape[0]
 
     token_float = tokens.astype(F32)
     inv = lax.rsqrt(jnp.mean(token_float * token_float, axis=1, keepdims=True) + EPSILON)
@@ -357,9 +408,16 @@
     live_mask = (slot_place < jnp.repeat(group_length, GROUP)).astype(BF16)[:, None]
     picked = cotangent * live_mask
     out_grad = jnp.dot(gnormed_low.T, picked, preferred_element_type=F32)
-    out_grad = lax.psum_scatter(out_grad, "dev", scatter_dimension=0, tiled=True)
+    out_grad = scatter_sums(out_grad.reshape((ndev,) + out_weight.shape), ndev, swapped, BF16)
     in_grad = jnp.dot(normed_low.T, grad_proj, preferred_element_type=F32)
-    in_grad = lax.psum_scatter(in_grad, "dev", scatter_dimension=0, tiled=True)
+    in_grad = in_grad.reshape(ndev, owned, width)
+    in_grad = jnp.concatenate(
+        [
+            scatter_sums(in_grad[:, :upper], ndev, plain, BF16),
+            scatter_sums(in_grad[:, upper:], ndev, swapped, BF16),
+        ],
+        axis=0,
+    )
     grad_normed = jnp.dot(grad_proj, in_w.T, preferred_element_type=F32)
     unit = token_float * inv
     grad_norm_g = jnp.sum(grad_normed * unit, axis=0)
@@ -376,11 +434,9 @@
         ],
         axis=1,
     )
-    width = small.shape[1]
     head_part = jnp.stack([dhead[0, :HEADS], jnp.sum(dskip.reshape(HEADS, HEAD_DIM), axis=1), dhead[2, :HEADS]])
-    total = lax.psum(jnp.concatenate([small.reshape(-1), head_part.reshape(-1)]), "dev")
-    head_total = total[ndev * width :].reshape(3, HEADS)
-    mine = lax.dynamic_slice(total, (lax.axis_index("dev") * width,), (width,))
+    head_total = sum_all(head_part, ndev)
+    mine = scatter_sums(small, ndev, plain, F32)
     cw_o, cb_o, ng_o, gg_o = jnp.split(mine, cuts)
     return (
         block_out,

time: 559 us -> 406 us (0.73)
  waiting for transfers between devices: 220 us -> 67.8 us
  blocking collectives: 82.3 us -> 0 us
  starting transfers between devices: 0.16 us -> 48.6 us
  local copies, waits for them, and re-layouts: 17.2 us -> 44.8 us
  other arithmetic: 10.1 us -> 29.5 us
  between operations: 14 us -> 1.77 us
  matrix products: 66.6 us -> 59.2 us
    unnamed x5 -> x0, waiting for transfers between devices: 150 us -> none
    ppermute x0 -> x40, waiting for transfers between devices: none -> 67.8 us  [the longest x20 34.3 us: scatter_sums(): blocks = kept + lax.ppermute(away, 'dev', partners(count, bit)).astype(F32)]
    all_gather x2 -> x0, waiting for transfers between devices: 53.6 us -> none  [the longest x1 36.8 us: body(): out_w = lax.all_gather(out_weight, 'dev', axis=0, tiled=True)]
    ppermute x0 -> x40, starting transfers between devices: none -> 48.6 us  [the longest x15 20.7 us: gather_blocks(): other = lax.ppermute(block, 'dev', partners(count, bit))]
    unnamed x1 -> x0, blocking collectives: 42.8 us -> none
    psum x1 -> x0, blocking collectives: 39.5 us -> none  [body(): lax.psum(jnp.concatenate([small.reshape(-1), head_part.reshape(-1)]), 'dev')]
    reduce_scatter x1 -> x0, waiting for transfers between devices: 16.7 us -> none  [body(): lax.psum_scatter(out_grad, 'dev', scatter_dimension=0, tiled=True)]
    add x0 -> x25, other arithmetic: none -> 8.69 us  [the longest x20 8.08 us: scatter_sums(): blocks = kept + lax.ppermute(away, 'dev', partners(count, bit)).astype(F32)]
  transfers between devices with their start and end apart: 4 -> 40, of which waited for: 4 -> 20; matrix products, arithmetic and copies ran while one was open for 15% -> 17% of each run, Pallas kernels for 0% -> 0%
where the time goes in v2:
time: 406 us; the launch traced here: 400 us
  Pallas kernels  149 us (37%)
  waiting for transfers between devices  67.8 us (17%)
  matrix products  59.2 us (15%)
  starting transfers between devices  48.6 us (12%)
  local copies, waits for them, and re-layouts  44.8 us (11%)
  other arithmetic  29.5 us (7%)
    pallas_call x1, Pallas kernels, run_pairs(): pl.pallas_call(pair_kernel, grid=(rows // PAIR,), in_specs=[smem, smem, r...  149 us
    ppermute x20, waiting for transfers between devices, scatter_sums(): blocks = kept + lax.ppermute(away, 'dev', partners(count, bit)).astype(F32)  34.3 us
    ppermute x15, waiting for transfers between devices, gather_blocks(): other = lax.ppermute(block, 'dev', partners(count, bit))  30.7 us
    ppermute x15, starting transfers between devices, gather_blocks(): other = lax.ppermute(block, 'dev', partners(count, bit))  20.7 us
    ppermute x20, starting transfers between devices, scatter_sums(): blocks = kept + lax.ppermute(away, 'dev', partners(count, bit)).astype(F32)  19.9 us
    dot_general x1, matrix products, body(): grad_normed = jnp.dot(grad_proj, in_w.T, preferred_element_type=F32)  19 us
    dot_general x1, matrix products, body(): in_grad = jnp.dot(normed_low.T, grad_proj, preferred_element_type=F32)  15.9 us
    dot_general x1, matrix products, body(): projected = jnp.dot(normed_low, in_w, preferred_element_type=F32)  15.7 us
  transfers between devices with their start and end apart: 40, of which 20 were waited for; matrix products, arithmetic and copies ran while one was open for 17% of the time, Pallas kernels for 0%

profile of v2, /device:TPU:0, one launch (start us, length us, event | category | flops | bytes accessed | tf_op | source)
XLA Modules:
  0.0 400.3 jit_solution(13221295754876193319)
XLA Ops:
  0.7 4.1 %collective-permute-start.10 = (bf16[48,768]{1,0:T(8,128)(2,1)}, bf16[48,768]{1,0:T(8,128)(2,1)S(1)}, u32[]{:S(2)}, u32[]{:S(2)}) collective-permute-start(bf16[48,768]{1,0:T(8,128)(2,1)} %param.14), channel_id=1, source_target_pairs={{0,16},{1,17},{2,18},{3,19},{4,20},{5,21},{6,22},{7,23},{8,24},{9,... | collective-permute-start | bytes 221192 | tf_op jit(solution)/shard_map/ppermute | solution.py:337
  8.4 2.9 collective-permute-start
  11.3 2.6 fusion.10
  16.6 1.6 collective-permute-start.1
  18.9 1.6 collective-permute-start.6
  20.5 2.0 collective-permute-done.1
  22.6 1.6 collective-permute-start.2
  24.2 1.5 collective-permute-done.11
  25.8 1.6 collective-permute-start.12
  27.3 1.5 collective-permute-done.6
  28.9 1.6 collective-permute-start.7
  30.9 1.6 collective-permute-start.3
  32.5 1.5 collective-permute-done.12
  34.0 1.6 collective-permute-start.13
  35.6 6.5 %collective-permute-done.7 = bf16[2,2,16,3352]{3,2,1,0:T(8,128)(2,1)S(1)} collective-permute-done((bf16[2,2,16,3352]{3,2,1,0:T(8,128)(2,1)S(1)}, bf16[2,2,16,3352]{3,2,1,0:T(8,128)(2,1)S(1)}, u32[]{:S(2)}, u32[]{:S(2)}) %collective-permute-start.7) | collective-permute-done | bytes 429088 | tf_op jit(solution)/shard_map/ppermute | solution.py:337
  42.3 1.6 collective-permute-start.8
  43.8 7.7 %collective-permute-done.3 = bf16[2,2,2,8,3396]{4,3,2,1,0:T(8,128)(2,1)S(1)} collective-permute-done((bf16[2,2,2,8,3396]{4,3,2,1,0:T(8,128)(2,1)S(1)}, bf16[2,2,2,8,3396]{4,3,2,1,0:T(8,128)(2,1)S(1)}, u32[]{:S(2)}, u32[]{:S(2)}) %collective-permute-start.3) | collective-permute-done | bytes 434720 | tf_op jit(solution)/shard_map/ppermute | solution.py:337
  51.8 9.8 %collective-permute-done.13 = bf16[2,2,2,48,768]{4,3,0,1,2:T(8,128)(2,1)S(1)} collective-permute-done((bf16[2,2,2,48,768]{4,3,0,1,2:T(8,128)(2,1)S(1)}, bf16[2,2,2,48,768]{4,3,0,1,2:T(8,128)(2,1)S(1)}, u32[]{:S(2)}, u32[]{:S(2)}) %collective-permute-start.13) | collective-permute-done | bytes 589856 | tf_op jit(solution)/shard_map/ppermute | solution.py:337
  63.3 1.4 pad_maximum_fusion.4
  66.2 1.6 reshape.139
  70.0 1.4 split.37
  71.4 1.4 split.38
  73.5 2.0 reshape.131
  75.5 2.1 copy.36
  77.5 1.4 reshape.132.cb_ref
  79.0 1.4 reshape.133.gg_ref
  80.4 1.8 select_bitcast_fusion.3
  82.3 1.7 copy.35
  84.0 1.8 select_bitcast_fusion.1
  86.7 2.8 copy-done
  89.4 15.7 %fusion.18.proj_ref = f32[2048,3352]{1,0:T(8,128)} fusion(bf16[768,3352]{1,0:T(8,128)(2,1)S(1)} %bitcast.188, bf16[2048,768]{1,0:T(8,128)(2,1)S(1)} %copy-done, f32[768]{0:T(1024)S(1)} %copy-done.13, f32[2048]{0:T(1024)S(1)} %copy-done.11), kind=kOutput, calls=%fused_computation.39 | convolution fusion | flops 10550771712 | bytes 35765248 | tf_op jit(solution)/shard_map/dot_general | solution.py:398
  107.5 148.6 %shard_map.178 = (bf16[2048,768]{1,0:T(8,128)(2,1)}, bf16[2048,1536]{1,0:T(8,128)(2,1)}, bf16[2048,3352]{1,0:T(8,128)(2,1)}, f32[4,1792]{1,0:T(4,128)}, f32[1,17...) custom-call(s32[8]{0:T(128)} %len_ref.1, s32[8]{0:T(128)} %first_ref.1, ...), custom_call_target="tpu_custom_call" | custom-call | tf_op jit(solution)/shard_map/pallas_call | solution.py:280
  256.1 19.0 %fusion.9 = (f32[768]{0:T(1024)S(1)}, f32[2048]{0:T(1024)S(1)}, f32[2048,768]{1,0:T(8,128)}) fusion(bf16[2048,768]{1,0:T(8,128)(2,1)S(1)} %copy-done.1, f32[2048]{0:T(1024)S(1)} %copy-done.11, f32[768]{0:T(1024)S(1)} %copy-done.13, bf16[2048,3352]{1,0:T(8,128)(2,1)} %get-tuple-element.18, bf16[768,3352]{1,0:T(8,128)(2,1)} %bitcast.189), kind=kOutput, calls=%fused_computation.11 | convolution fusion | flops 10555487232 | bytes 28338176 | tf_op jit(solution)/shard_map/dot_general | solution.py:421
  275.1 15.9 %fusion.16 = f32[768,3352]{1,0:T(8,128)S(1)} fusion(bf16[2048,3352]{1,0:T(8,128)(2,1)} %get-tuple-element.18, bf16[2048,768]{1,0:T(8,128)(2,1)S(1)} %copy-done.1, f32[768]{0:T(1024)S(1)} %copy-done.13, f32[2048]{0:T(1024)S(1)} %copy-done.11), kind=kOutput, calls=%fused_computation.38 | convolution fusion | flops 10550771712 | bytes 27184128 | tf_op jit(solution)/shard_map/dot_general | solution.py:412
  290.9 3.3 slice.51
  294.3 2.1 slice.52
  299.0 1.6 concatenate.28
  301.5 8.7 %fusion.11 = f32[1536,768]{1,0:T(8,128)S(1)} fusion(bf16[2048,1536]{1,0:T(8,128)(2,1)} %get-tuple-element.19, bf16[2048,768]{1,0:T(8,128)(2,1)} %cot_ref.1, bf16[2048]{0:T(1024)(128)(2,1)S(1)} %copy-done.17), kind=kOutput, calls=%fused_computation.17 | convolution fusion | flops 4833411072 | bytes 14159872 | tf_op jit(solution)/shard_map/dot_general | solution.py:410
  312.2 1.6 collective-permute-start.36
  314.5 1.4 collective-permute-done.36
  315.9 1.6 collective-permute-start.37
  317.7 1.6 collective-permute-start.32
  319.3 3.4 fusion.13
  324.9 1.4 collective-permute-done.38
  326.4 3.6 collective-permute-start.39
  330.0 1.6 collective-permute-start.34
  334.4 5.5 %fusion.8 = f32[2048,768]{1,0:T(8,128)} fusion(bf16[2048,768]{1,0:T(8,128)(2,1)S(1)} %copy-done.1, bf16[2048,768]{1,0:T(8,128)(2,1)S(1)} %copy-done.2, f32[2048,768]{1,0:T(8,128)} %get-tuple-element.78, f32[2048]{0:T(1024)S(1)} %broadcast_multiply_fusion, f32[768]{0:T(1024)S(1)} %copy-done.13, f32[2048]{0:T(1024)S(1)} %copy-done.11), kind=kLoop, calls=%fused_computation.10 | loop fusion | flops 12582912 | bytes 18893824 | tf_op jit(solution)/shard_map/add | solution.py:426
  343.0 2.0 collective-permute-done.21
  347.0 2.3 bitcast_add_fusion.1
  349.4 1.4 collective-permute-start.26
  350.8 1.6 collective-permute-done.22
  353.2 2.9 bitcast_add_fusion
  358.0 1.5 collective-permute-start.24
  359.4 2.8 collective-permute-done.26
  362.4 1.6 collective-permute-start.27
  364.0 13.4 %collective-permute-done.16 = bf16[2,2,2,16,3352]{4,3,2,1,0:T(8,128)(2,1)S(1)} collective-permute-done((bf16[2,2,2,16,3352]{4,3,2,1,0:T(8,128)(2,1)S(1)}, bf16[2,2,2,16,3352]{4,3,2,1,0:T(8,128)(2,1)S(1)}, u32[]{:S(2)}, u32[]{:S(2)}) %collective-permute-start.16) | collective-permute-done | bytes 858144 | tf_op jit(solution)/shard_map/ppermute | solution.py:353
  378.2 2.3 collective-permute-done.27
  380.6 1.5 collective-permute-start.28
  382.1 3.9 collective-permute-done.17
  386.1 1.5 collective-permute-start.18
  387.7 1.5 collective-permute-start.29
  389.1 3.0 collective-permute-done.18
  392.2 2.3 collective-permute-start.19
  395.1 3.9 collective-permute-done.19
  (195 shorter events, 39.3 us)
Async XLA Ops:
  0.6 17.6 %copy-start.10 = (bf16[48,768]{1,0:T(8,128)(2,1)S(1)}, bf16[48,768]{1,0:T(8,128)(2,1)}, u32[]{:S(2)}) copy-start(bf16[48,768]{1,0:T(8,128)(2,1)} %param.14) | copy-start | bytes 221188
  0.7 18.2 %copy-start.9 = (bf16[24,3352]{1,0:T(8,128)(2,1)S(1)}, bf16[24,3352]{1,0:T(8,128)(2,1)}, u32[]{:S(2)}) copy-start(bf16[24,3352]{1,0:T(8,128)(2,1)} %param.13) | copy-start | bytes 482692
  0.7 13.8 %copy-start.19 = (s32[8]{0:T(128)S(1)}, s32[8]{0:T(128)}, u32[]{:S(2)}) copy-start(s32[8]{0:T(128)} %len_ref.1) | copy-start | bytes 100
  0.7 14.5 %copy-start.18 = (f32[3,24]{1,0:T(4,128)S(1)}, f32[3,24]{1,0:T(4,128)}, u32[]{:S(2)}) copy-start(f32[3,24]{1,0:T(4,128)} %param.19) | copy-start | bytes 868
  0.7 17.6 %collective-permute-start.10 = (bf16[48,768]{1,0:T(8,128)(2,1)}, bf16[48,768]{1,0:T(8,128)(2,1)S(1)}, u32[]{:S(2)}, u32[]{:S(2)}) collective-permute-start(bf16[48,768]{1,0:T(8,128)(2,1)} %param.14), channel_id=1, source_target_pairs={{0,16},{1,17},{2,18},{3,19},{4,20},{5,21},{6,22},{7,23},{8,24},{9,... | collective-permute-start | bytes 221192 | tf_op jit(solution)/shard_map/ppermute | solution.py:337
  5.7 13.1 %collective-permute-start.5 = (bf16[16,3352]{1,0:T(8,128)(2,1)S(1)}, bf16[16,3352]{1,0:T(8,128)(2,1)S(1)}, u32[]{:S(2)}, u32[]{:S(2)}) collective-permute-start(bf16[16,3352]{1,0:T(8,128)(2,1)S(1)} %slice.40), channel_id=1, source_target_pairs={{0,16},{1,17},{2,18},{3,19},{4,20},{5,21},{6,22},{7,23},{8,24},{9,... | collective-permute-start | bytes 321800 | tf_op jit(solution)/shard_map/ppermute | solution.py:337
  8.4 8.1 %collective-permute-start = (bf16[8,3396]{1,0:T(8,128)(2,1)S(1)}, bf16[8,3396]{1,0:T(8,128)(2,1)S(1)}, u32[]{:S(2)}, u32[]{:S(2)}) collective-permute-start(bf16[8,3396]{1,0:T(8,128)(2,1)S(1)} %pad_maximum_fusion.17), channel_id=1, source_target_pairs={{0,16},{1,17},{2,18},{3,19},{4,20},{5,21},{6,22},{7,23},{8,24},{9,... | collective-permute-start | bytes 163016 | tf_op jit(solution)/shard_map/ppermute | solution.py:337
  16.6 5.9 %collective-permute-start.1 = (bf16[2,8,3396]{2,1,0:T(8,128)(2,1)S(1)}, bf16[2,8,3396]{2,1,0:T(8,128)(2,1)S(1)}, u32[]{:S(2)}, u32[]{:S(2)}) collective-permute-start(bf16[2,8,3396]{2,1,0:T(8,128)(2,1)S(1)} %pad_maximum_fusion.16), channel_id=1, source_target_pairs={{0,8},{1,9},{2,10},{3,11},{4,12},{5,13},{6,14},{7,15},{8,0},{9,1},... | collective-permute-start | bytes 326024 | tf_op jit(solution)/shard_map/ppermute | solution.py:337
  18.3 7.4 %collective-permute-start.11 = (bf16[2,48,768]{2,1,0:T(8,128)(2,1)S(1)}, bf16[2,48,768]{2,1,0:T(8,128)(2,1)S(1)}, u32[]{:S(2)}, u32[]{:S(2)}) collective-permute-start(bf16[2,48,768]{2,1,0:T(8,128)(2,1)S(1)} %pad_maximum_fusion.15), channel_id=1, source_target_pairs={{0,8},{1,9},{2,10},{3,11},{4,12},{5,13},{6,14},{7,15},{8,0},{9,1},... | collective-permute-start | bytes 442376 | tf_op jit(solution)/shard_map/ppermute | solution.py:337
  18.9 9.9 %collective-permute-start.6 = (bf16[2,16,3352]{2,1,0:T(8,128)(2,1)S(1)}, bf16[2,16,3352]{2,1,0:T(8,128)(2,1)S(1)}, u32[]{:S(2)}, u32[]{:S(2)}) collective-permute-start(bf16[2,16,3352]{2,1,0:T(8,128)(2,1)S(1)} %pad_maximum_fusion.14), channel_id=1, source_target_pairs={{0,8},{1,9},{2,10},{3,11},{4,12},{5,13},{6,14},{7,15},{8,0},{9,1},... | collective-permute-start | bytes 643592 | tf_op jit(solution)/shard_map/ppermute | solution.py:337
  22.6 8.1 %collective-permute-start.2 = (bf16[2,2,8,3396]{3,2,1,0:T(8,128)(2,1)S(1)}, bf16[2,2,8,3396]{3,2,1,0:T(8,128)(2,1)S(1)}, u32[]{:S(2)}, u32[]{:S(2)}) collective-permute-start(bf16[2,2,8,3396]{3,2,1,0:T(8,128)(2,1)S(1)} %pad_maximum_fusion.13), channel_id=1, source_target_pairs={{0,2},{1,3},{2,0},{3,1},{4,6},{5,7},{6,4},{7,5},{8,10},{9,11},{10,... | collective-permute-start | bytes 652040 | tf_op jit(solution)/shard_map/ppermute | solution.py:337
  25.8 8.1 %collective-permute-start.12 = (bf16[2,2,48,768]{3,2,0,1:T(8,128)(2,1)S(1)}, bf16[2,2,48,768]{3,2,0,1:T(8,128)(2,1)S(1)}, u32[]{:S(2)}, u32[]{:S(2)}) collective-permute-start(bf16[2,2,48,768]{3,2,0,1:T(8,128)(2,1)S(1)} %pad_maximum_fusion.12), channel_id=1, source_target_pairs={{0,2},{1,3},{2,0},{3,1},{4,6},{5,7},{6,4},{7,5},{8,10},{9,11},{10,... | collective-permute-start | bytes 884744 | tf_op jit(solution)/shard_map/ppermute | solution.py:337
  28.9 13.2 %collective-permute-start.7 = (bf16[2,2,16,3352]{3,2,1,0:T(8,128)(2,1)S(1)}, bf16[2,2,16,3352]{3,2,1,0:T(8,128)(2,1)S(1)}, u32[]{:S(2)}, u32[]{:S(2)}) collective-permute-start(bf16[2,2,16,3352]{3,2,1,0:T(8,128)(2,1)S(1)} %pad_maximum_fusion.10), channel_id=1, source_target_pairs={{0,4},{1,5},{2,6},{3,7},{4,0},{5,1},{6,2},{7,3},{8,12},{9,13},{10,... | collective-permute-start | bytes 1287176 | tf_op jit(solution)/shard_map/ppermute | solution.py:337
  30.9 20.7 %collective-permute-start.3 = (bf16[2,2,2,8,3396]{4,3,2,1,0:T(8,128)(2,1)S(1)}, bf16[2,2,2,8,3396]{4,3,2,1,0:T(8,128)(2,1)S(1)}, u32[]{:S(2)}, u32[]{:S(2)}) collective-permute-start(bf16[2,2,2,8,3396]{4,3,2,1,0:T(8,128)(2,1)S(1)} %pad_maximum_fusion.9), channel_id=1, source_target_pairs={{0,4},{1,5},{2,6},{3,7},{4,0},{5,1},{6,2},{7,3},{8,12},{9,13},{10,... | collective-permute-start | bytes 1304072 | tf_op jit(solution)/shard_map/ppermute | solution.py:337
  34.0 27.6 %collective-permute-start.13 = (bf16[2,2,2,48,768]{4,3,0,1,2:T(8,128)(2,1)S(1)}, bf16[2,2,2,48,768]{4,3,0,1,2:T(8,128)(2,1)S(1)}, u32[]{:S(2)}, u32[]{:S(2)}) collective-permute-start(bf16[2,2,2,48,768]{4,3,0,1,2:T(8,128)(2,1)S(1)} %pad_maximum_fusion.8), channel_id=1, source_target_pairs={{0,4},{1,5},{2,6},{3,7},{4,0},{5,1},{6,2},{7,3},{8,12},{9,13},{10,... | collective-permute-start | bytes 1769480 | tf_op jit(solution)/shard_map/ppermute | solution.py:337
  42.3 20.9 %collective-permute-start.8 = (bf16[2,2,2,16,3352]{4,3,2,1,0:T(8,128)(2,1)S(1)}, bf16[2,2,2,16,3352]{4,3,2,1,0:T(8,128)(2,1)S(1)}, u32[]{:S(2)}, u32[]{:S(2)}) collective-permute-start(bf16[2,2,2,16,3352]{4,3,2,1,0:T(8,128)(2,1)S(1)} %pad_maximum_fusion.7), channel_id=1, source_target_pairs={{0,2},{1,3},{2,0},{3,1},{4,6},{5,7},{6,4},{7,5},{8,10},{9,11},{10,... | collective-permute-start | bytes 2574344 | tf_op jit(solution)/shard_map/ppermute | solution.py:337
  51.8 13.3 %collective-permute-start.4 = (bf16[2,2,2,2,8,3396]{5,4,3,2,1,0:T(8,128)(2,1)S(1)}, bf16[2,2,2,2,8,3396]{5,4,3,2,1,0:T(8,128)(2,1)S(1)}, u32[]{:S(2)}, u32[]{:S(2)}) collective-permute-start(bf16[2,2,2,2,8,3396]{5,4,3,2,1,0:T(8,128)(2,1)S(1)} %pad_maximum_fusion.6), channel_id=1, source_target_pairs={{0,1},{1,0},{2,3},{3,2},{4,5},{5,4},{6,7},{7,6},{8,9},{9,8},{10,11... | collective-permute-start | bytes 2608136 | tf_op jit(solution)/shard_map/ppermute | solution.py:337
  61.7 1.3 copy-start.5
  61.7 1.4 copy-start.6
  62.9 17.4 %collective-permute-start.14 = (bf16[2,2,2,2,48,768]{5,4,0,1,3,2:T(8,128)(2,1)}, bf16[2,2,2,2,48,768]{5,4,0,1,3,2:T(8,128)(2,1)}, u32[]{:S(2)}, u32[]{:S(2)}) collective-permute-start(bf16[2,2,2,2,48,768]{5,4,0,1,3,2:T(8,128)(2,1)} %pad_maximum_fusion.5), channel_id=1, source_target_pairs={{0,1},{1,0},{2,3},{3,2},{4,5},{5,4},{6,7},{7,6},{8,9},{9,8},{10,11... | collective-permute-start | bytes 3538952 | tf_op jit(solution)/shard_map/ppermute | solution.py:337
  64.7 19.3 %collective-permute-start.9 = (bf16[2,2,2,2,16,3352]{5,4,3,2,1,0:T(8,128)(2,1)}, bf16[2,2,2,2,16,3352]{5,4,3,2,1,0:T(8,128)(2,1)}, u32[]{:S(2)}, u32[]{:S(2)}) collective-permute-start(bf16[2,2,2,2,16,3352]{5,4,3,2,1,0:T(8,128)(2,1)} %pad_maximum_fusion.4), channel_id=1, source_target_pairs={{0,1},{1,0},{2,3},{3,2},{4,5},{5,4},{6,7},{7,6},{8,9},{9,8},{10,11... | collective-permute-start | bytes 5148680 | tf_op jit(solution)/shard_map/ppermute | solution.py:337
  86.2 3.2 copy-start
  86.3 3.2 copy-start.11
  86.3 3.2 copy-start.13
  86.7 18.5 %copy-start.7 = (bf16[32,24,3352]{2,1,0:T(8,128)(2,1)}, bf16[32,24,3352]{2,1,0:T(8,128)(2,1)S(1)}, u32[]{:S(2)}) copy-start(bf16[32,24,3352]{2,1,0:T(8,128)(2,1)S(1)} %pad_maximum_fusion) | copy-start | bytes 15446020
  107.5 148.6 %copy-start.1 = (bf16[2048,768]{1,0:T(8,128)(2,1)S(1)}, bf16[2048,768]{1,0:T(8,128)(2,1)}, u32[]{:S(2)}) copy-start(bf16[2048,768]{1,0:T(8,128)(2,1)} %tok_ref.1) | copy-start | bytes 9437188
  294.3 2.1 copy-start.16
  294.3 3.4 copy-start.12
  294.3 6.3 %copy-start.14 = (f32[1,1792]{1,0:T(1,128)S(1)}, f32[1,1792]{1,0:T(1,128)}, u32[]{:S(2)}) copy-start(f32[1,1792]{1,0:T(1,128)} %get-tuple-element.21) | copy-start | bytes 21508
  294.3 6.4 %copy-start.15 = (f32[1,1536]{1,0:T(1,128)S(1)}, f32[1,1536]{1,0:T(1,128)}, u32[]{:S(2)}) copy-start(f32[1,1536]{1,0:T(1,128)} %get-tuple-element.22) | copy-start | bytes 18436
  294.3 7.2 %copy-start.17 = (bf16[2048]{0:T(1024)(128)(2,1)S(1)}, bf16[2048]{0:T(1024)(128)(2,1)}, u32[]{:S(2)}) copy-start(bf16[2048]{0:T(1024)(128)(2,1)} %fusion.37) | copy-start | bytes 12292
  297.3 14.9 %collective-permute-start.35 = (f32[3,24]{1,0:T(4,128)S(1)}, f32[3,24]{1,0:T(4,128)S(1)}, u32[]{:S(2)}, u32[]{:S(2)}) collective-permute-start(f32[3,24]{1,0:T(4,128)S(1)} %pad_maximum_fusion.19), channel_id=1, source_target_pairs={{0,1},{1,0},{2,3},{3,2},{4,5},{5,4},{6,7},{7,6},{8,9},{9,8},{10,11... | collective-permute-start | bytes 872 | tf_op jit(solution)/shard_map/ppermute | solution.py:360
  301.1 12.7 %collective-permute-start.30 = (f32[2,2,2,2,352]{4,3,2,1,0:T(2,128)S(1)}, f32[2,2,2,2,352]{4,3,2,1,0:T(2,128)S(1)}, u32[]{:S(2)}, u32[]{:S(2)}) collective-permute-start(f32[2,2,2,2,352]{4,3,2,1,0:T(2,128)S(1)} %bitcast.195), channel_id=1, source_target_pairs={{0,1},{1,0},{2,3},{3,2},{4,5},{5,4},{6,7},{7,6},{8,9},{9,8},{10,11... | collective-permute-start | bytes 67592 | tf_op jit(solution)/shard_map/ppermute | solution.py:353
  301.5 10.2 %copy-start.3 = (f32[32,8,3352]{2,1,0:T(8,128)S(1)}, f32[32,8,3352]{2,1,0:T(8,128)}, u32[]{:S(2)}) copy-start(f32[32,8,3352]{2,1,0:T(8,128)} %slice.52) | copy-start | bytes 10297348
  310.2 9.1 %copy-start.8 = (f32[1536,768]{1,0:T(8,128)}, f32[1536,768]{1,0:T(8,128)S(1)}, u32[]{:S(2)}) copy-start(f32[1536,768]{1,0:T(8,128)S(1)} %fusion.11) | copy-start | bytes 14155780
  311.5 35.5 %collective-permute-start.25 = (bf16[2,2,2,2,48,768]{5,4,0,1,3,2:T(8,128)(2,1)}, bf16[2,2,2,2,48,768]{5,4,0,1,3,2:T(8,128)(2,1)}, u32[]{:S(2)}, u32[]{:S(2)}) collective-permute-start(bf16[2,2,2,2,48,768]{5,4,0,1,3,2:T(8,128)(2,1)} %fusion.15), channel_id=1, source_target_pairs={{0,1},{1,0},{2,3},{3,2},{4,5},{5,4},{6,7},{7,6},{8,9},{9,8},{10,11... | collective-permute-start | bytes 3538952 | tf_op jit(solution)/shard_map/ppermute | solution.py:353
  311.8 19.8 %collective-permute-start.20 = (bf16[2,2,2,2,8,3352]{5,4,0,1,3,2:T(8,128)(2,1)S(1)}, bf16[2,2,2,2,8,3352]{5,4,0,1,3,2:T(8,128)(2,1)S(1)}, u32[]{:S(2)}, u32[]{:S(2)}) collective-permute-start(bf16[2,2,2,2,8,3352]{5,4,0,1,3,2:T(8,128)(2,1)S(1)} %fusion.21), channel_id=1, source_target_pairs={{0,1},{1,0},{2,3},{3,2},{4,5},{5,4},{6,7},{7,6},{8,9},{9,8},{10,11... | collective-permute-start | bytes 2574344 | tf_op jit(solution)/shard_map/ppermute | solution.py:353
  312.2 3.7 collective-permute-start.36
  313.9 3.8 collective-permute-start.31
  315.9 6.8 %collective-permute-start.37 = (f32[3,24]{1,0:T(4,128)S(1)}, f32[3,24]{1,0:T(4,128)S(1)}, u32[]{:S(2)}, u32[]{:S(2)}) collective-permute-start(f32[3,24]{1,0:T(4,128)S(1)} %fusion.47), channel_id=1, source_target_pairs={{0,4},{1,5},{2,6},{3,7},{4,0},{5,1},{6,2},{7,3},{8,12},{9,13},{10,... | collective-permute-start | bytes 872 | tf_op jit(solution)/shard_map/ppermute | solution.py:360
  317.7 6.1 %collective-permute-start.32 = (f32[2,2,352]{2,1,0:T(2,128)S(1)}, f32[2,2,352]{2,1,0:T(2,128)S(1)}, u32[]{:S(2)}, u32[]{:S(2)}) collective-permute-start(f32[2,2,352]{2,1,0:T(2,128)S(1)} %bitcast.200), channel_id=1, source_target_pairs={{0,4},{1,5},{2,6},{3,7},{4,0},{5,1},{6,2},{7,3},{8,12},{9,13},{10,... | collective-permute-start | bytes 16904 | tf_op jit(solution)/shard_map/ppermute | solution.py:353
  322.7 11.7 %copy-start.2 = (bf16[2048,768]{1,0:T(8,128)(2,1)S(1)}, bf16[2048,768]{1,0:T(8,128)(2,1)}, u32[]{:S(2)}) copy-start(bf16[2048,768]{1,0:T(8,128)(2,1)} %cot_ref.1) | copy-start | bytes 9437188
  322.7 30.5 %collective-permute-start.15 = (bf16[2,2,2,2,16,3352]{5,4,3,2,1,0:T(8,128)(2,1)}, bf16[2,2,2,2,16,3352]{5,4,3,2,1,0:T(8,128)(2,1)}, u32[]{:S(2)}, u32[]{:S(2)}) collective-permute-start(bf16[2,2,2,2,16,3352]{5,4,3,2,1,0:T(8,128)(2,1)} %fusion.13), channel_id=1, source_target_pairs={{0,1},{1,0},{2,3},{3,2},{4,5},{5,4},{6,7},{7,6},{8,9},{9,8},{10,11... | collective-permute-start | bytes 5148680 | tf_op jit(solution)/shard_map/ppermute | solution.py:353
  322.7 3.7 collective-permute-start.38
  323.8 6.2 %collective-permute-start.33 = (f32[2,352]{1,0:T(2,128)S(1)}, f32[2,352]{1,0:T(2,128)S(1)}, u32[]{:S(2)}, u32[]{:S(2)}) collective-permute-start(f32[2,352]{1,0:T(2,128)S(1)} %bitcast.201), channel_id=1, source_target_pairs={{0,8},{1,9},{2,10},{3,11},{4,12},{5,13},{6,14},{7,15},{8,0},{9,1},... | collective-permute-start | bytes 8456 | tf_op jit(solution)/shard_map/ppermute | solution.py:353
  326.4 13.6 %collective-permute-start.39 = (f32[3,24]{1,0:T(4,128)S(1)}, f32[3,24]{1,0:T(4,128)S(1)}, u32[]{:S(2)}, u32[]{:S(2)}) collective-permute-start(f32[3,24]{1,0:T(4,128)S(1)} %add.225), channel_id=1, source_target_pairs={{0,16},{1,17},{2,18},{3,19},{4,20},{5,21},{6,22},{7,23},{8,24},{9,... | collective-permute-start | bytes 872 | tf_op jit(solution)/shard_map/ppermute | solution.py:360
  330.0 10.5 %collective-permute-start.34 = (f32[352]{0:T(512)S(1)}, f32[352]{0:T(512)S(1)}, u32[]{:S(2)}, u32[]{:S(2)}) collective-permute-start(f32[352]{0:T(512)S(1)} %get-tuple-element.36), channel_id=1, source_target_pairs={{0,16},{1,17},{2,18},{3,19},{4,20},{5,21},{6,22},{7,23},{8,24},{9,... | collective-permute-start | bytes 4232 | tf_op jit(solution)/shard_map/ppermute | solution.py:353
  331.8 1.2 copy-start.4
  333.9 11.1 %collective-permute-start.21 = (bf16[2,2,2,8,3352]{4,3,0,1,2:T(8,128)(2,1)}, bf16[2,2,2,8,3352]{4,3,0,1,2:T(8,128)(2,1)}, u32[]{:S(2)}, u32[]{:S(2)}) collective-permute-start(bf16[2,2,2,8,3352]{4,3,0,1,2:T(8,128)(2,1)} %fusion.24), channel_id=1, source_target_pairs={{0,4},{1,5},{2,6},{3,7},{4,0},{5,1},{6,2},{7,3},{8,12},{9,13},{10,... | collective-permute-start | bytes 1287176 | tf_op jit(solution)/shard_map/ppermute | solution.py:353
  346.4 6.0 %collective-permute-start.22 = (bf16[2,2,8,3352]{3,2,0,1:T(8,128)(2,1)S(1)}, bf16[2,2,8,3352]{3,2,0,1:T(8,128)(2,1)S(1)}, u32[]{:S(2)}, u32[]{:S(2)}) collective-permute-start(bf16[2,2,8,3352]{3,2,0,1:T(8,128)(2,1)S(1)} %fusion.27), channel_id=1, source_target_pairs={{0,2},{1,3},{2,0},{3,1},{4,6},{5,7},{6,4},{7,5},{8,10},{9,11},{10,... | collective-permute-start | bytes 643592 | tf_op jit(solution)/shard_map/ppermute | solution.py:353
  349.4 12.8 %collective-permute-start.26 = (bf16[2,2,2,48,768]{4,3,0,1,2:T(8,128)(2,1)S(1)}, bf16[2,2,2,48,768]{4,3,0,1,2:T(8,128)(2,1)S(1)}, u32[]{:S(2)}, u32[]{:S(2)}) collective-permute-start(bf16[2,2,2,48,768]{4,3,0,1,2:T(8,128)(2,1)S(1)} %fusion.22), channel_id=1, source_target_pairs={{0,4},{1,5},{2,6},{3,7},{4,0},{5,1},{6,2},{7,3},{8,12},{9,13},{10,... | collective-permute-start | bytes 1769480 | tf_op jit(solution)/shard_map/ppermute | solution.py:353
  352.5 5.4 %collective-permute-start.23 = (bf16[2,8,3352]{2,1,0:T(8,128)(2,1)S(1)}, bf16[2,8,3352]{2,1,0:T(8,128)(2,1)S(1)}, u32[]{:S(2)}, u32[]{:S(2)}) collective-permute-start(bf16[2,8,3352]{2,1,0:T(8,128)(2,1)S(1)} %fusion.30), channel_id=1, source_target_pairs={{0,8},{1,9},{2,10},{3,11},{4,12},{5,13},{6,14},{7,15},{8,0},{9,1},... | collective-permute-start | bytes 321800 | tf_op jit(solution)/shard_map/ppermute | solution.py:353
  356.2 21.2 %collective-permute-start.16 = (bf16[2,2,2,16,3352]{4,3,2,1,0:T(8,128)(2,1)S(1)}, bf16[2,2,2,16,3352]{4,3,2,1,0:T(8,128)(2,1)S(1)}, u32[]{:S(2)}, u32[]{:S(2)}) collective-permute-start(bf16[2,2,2,16,3352]{4,3,2,1,0:T(8,128)(2,1)S(1)} %fusion.20), channel_id=1, source_target_pairs={{0,2},{1,3},{2,0},{3,1},{4,6},{5,7},{6,4},{7,5},{8,10},{9,11},{10,... | collective-permute-start | bytes 2574344 | tf_op jit(solution)/shard_map/ppermute | solution.py:353
  358.0 20.2 %collective-permute-start.24 = (bf16[8,3352]{1,0:T(8,128)(2,1)S(1)}, bf16[8,3352]{1,0:T(8,128)(2,1)S(1)}, u32[]{:S(2)}, u32[]{:S(2)}) collective-permute-start(bf16[8,3352]{1,0:T(8,128)(2,1)S(1)} %fusion.32), channel_id=1, source_target_pairs={{0,16},{1,17},{2,18},{3,19},{4,20},{5,21},{6,22},{7,23},{8,24},{9,... | collective-permute-start | bytes 160904 | tf_op jit(solution)/shard_map/ppermute | solution.py:353
  362.4 18.1 %collective-permute-start.27 = (bf16[2,2,48,768]{3,2,0,1:T(8,128)(2,1)S(1)}, bf16[2,2,48,768]{3,2,0,1:T(8,128)(2,1)S(1)}, u32[]{:S(2)}, u32[]{:S(2)}) collective-permute-start(bf16[2,2,48,768]{3,2,0,1:T(8,128)(2,1)S(1)} %fusion.25), channel_id=1, source_target_pairs={{0,2},{1,3},{2,0},{3,1},{4,6},{5,7},{6,4},{7,5},{8,10},{9,11},{10,... | collective-permute-start | bytes 884744 | tf_op jit(solution)/shard_map/ppermute | solution.py:353
  377.6 8.4 %collective-permute-start.17 = (bf16[2,2,16,3352]{3,2,1,0:T(8,128)(2,1)S(1)}, bf16[2,2,16,3352]{3,2,1,0:T(8,128)(2,1)S(1)}, u32[]{:S(2)}, u32[]{:S(2)}) collective-permute-start(bf16[2,2,16,3352]{3,2,1,0:T(8,128)(2,1)S(1)} %fusion.23), channel_id=1, source_target_pairs={{0,4},{1,5},{2,6},{3,7},{4,0},{5,1},{6,2},{7,3},{8,12},{9,13},{10,... | collective-permute-start | bytes 1287176 | tf_op jit(solution)/shard_map/ppermute | solution.py:353
  380.6 7.0 %collective-permute-start.28 = (bf16[2,48,768]{2,1,0:T(8,128)(2,1)S(1)}, bf16[2,48,768]{2,1,0:T(8,128)(2,1)S(1)}, u32[]{:S(2)}, u32[]{:S(2)}) collective-permute-start(bf16[2,48,768]{2,1,0:T(8,128)(2,1)S(1)} %fusion.28), channel_id=1, source_target_pairs={{0,8},{1,9},{2,10},{3,11},{4,12},{5,13},{6,14},{7,15},{8,0},{9,1},... | collective-permute-start | bytes 442376 | tf_op jit(solution)/shard_map/ppermute | solution.py:353
  386.1 6.0 %collective-permute-start.18 = (bf16[2,16,3352]{2,1,0:T(8,128)(2,1)S(1)}, bf16[2,16,3352]{2,1,0:T(8,128)(2,1)S(1)}, u32[]{:S(2)}, u32[]{:S(2)}) collective-permute-start(bf16[2,16,3352]{2,1,0:T(8,128)(2,1)S(1)} %fusion.26), channel_id=1, source_target_pairs={{0,8},{1,9},{2,10},{3,11},{4,12},{5,13},{6,14},{7,15},{8,0},{9,1},... | collective-permute-start | bytes 643592 | tf_op jit(solution)/shard_map/ppermute | solution.py:353
  387.7 6.8 %collective-permute-start.29 = (bf16[48,768]{1,0:T(8,128)(2,1)S(1)}, bf16[48,768]{1,0:T(8,128)(2,1)S(1)}, u32[]{:S(2)}, u32[]{:S(2)}) collective-permute-start(bf16[48,768]{1,0:T(8,128)(2,1)S(1)} %fusion.31), channel_id=1, source_target_pairs={{0,16},{1,17},{2,18},{3,19},{4,20},{5,21},{6,22},{7,23},{8,24},{9,... | collective-permute-start | bytes 221192 | tf_op jit(solution)/shard_map/ppermute | solution.py:353
  392.2 6.9 %collective-permute-start.19 = (bf16[16,3352]{1,0:T(8,128)(2,1)S(1)}, bf16[16,3352]{1,0:T(8,128)(2,1)S(1)}, u32[]{:S(2)}, u32[]{:S(2)}) collective-permute-start(bf16[16,3352]{1,0:T(8,128)(2,1)S(1)} %fusion.29), channel_id=1, source_target_pairs={{0,16},{1,17},{2,18},{3,19},{4,20},{5,21},{6,22},{7,23},{8,24},{9,... | collective-permute-start | bytes 321800 | tf_op jit(solution)/shard_map/ppermute | solution.py:353
